TPU v7x, 32 devices: a whole 2x2x4 slice. The times are simulated.
32 devices in a mesh: experts: 4 (over y, x), context: 4 (over z), dp: 2 (over core).
Axes of the slice: x: 2, y: 2, z: 4, core: 2. Of those that a mesh axis runs over, the one named last changes fastest.
Arguments:
- inputs: bfloat16 [2, 8, 1024, 768], P(None, ('experts', 'dp'), 'context'), may hold values from -6 to 6
- cotangent: bfloat16 [2, 8, 1024, 768], P(None, ('experts', 'dp'), 'context'), may hold values from -6 to 6
- qkv_weight: bfloat16 [3, 768, 768], P(None, ('context', 'dp')), may hold values from -0.21875 to 0.21875
- out_weight: bfloat16 [768, 768], P(('context', 'dp')), may hold values from -0.875 to 0.875
- norm_gains: float32 [2, 768], P(None, ('context', 'dp')), may hold values from 0.5 to 1.5
- route_weight: bfloat16 [768, 8], P(('context', 'dp')), may hold values from -0.109375 to 0.109375
- const_gate: bfloat16 [768, 4], P(('context', 'dp')), may hold values from -0.21875 to 0.21875
- const_vec: float32 [2, 768], P(None, ('context', 'dp')), may hold values from -6 to 6
- w_gate: bfloat16 [4, 768, 2048], P('experts', None, ('context', 'dp')), may hold values from -0.3125 to 0.3125
- w_up: bfloat16 [4, 768, 2048], P('experts', None, ('context', 'dp')), may hold values from -0.3125 to 0.3125
- w_down: bfloat16 [4, 768, 2048], P('experts', None, ('context', 'dp')), may hold values from -0.375 to 0.375
- prev_logits: float32 [2, 8, 1024, 8], P(None, ('experts', 'dp'), 'context'), may hold values from -3 to 3
- routes: int32 [2, 8, 1024, 2], P(None, ('experts', 'dp'), 'context'), may hold values from 0 to 7, all different within a row; in each aligned block of 256 rows (0 to 255, 256 to 511, ..., all dimensions but the last counted through in order) at most 80 rows name the same one
- segments: int32 [2, 8, 1024], P(None, ('experts', 'dp'), 'context'), may hold values from 0 to 6, as said below
Outputs:
- output: bfloat16 [2, 8, 1024, 768], P(None, ('experts', 'dp'), 'context')
- input_grad: float32 [2, 8, 1024, 768], P(None, ('experts', 'dp'), 'context')
- logit_grad: float32 [2, 8, 1024, 8], P(None, ('experts', 'dp'), 'context')
- qkv_grad: float32 [3, 768, 768], P(None, ('context', 'dp'))
- out_proj_grad: float32 [768, 768], P(('context', 'dp'))
- gain_grad: float32 [2, 768], P(None, ('context', 'dp'))
- route_grad: float32 [768, 8], P(('context', 'dp'))
- const_gate_grad: float32 [768, 4], P(('context', 'dp'))
- const_vec_grad: float32 [2, 768], P(None, ('context', 'dp'))
- gate_grad: float32 [4, 768, 2048], P('experts', None, ('context', 'dp'))
- up_grad: float32 [4, 768, 2048], P('experts', None, ('context', 'dp'))
- down_grad: float32 [4, 768, 2048], P('experts', None, ('context', 'dp'))
Inputs may be any that keep to these rules, and one draw needn't show every extreme that they name: `routes`: each row names two different experts; within the 256 positions of one sequence block, no expert is named more than 80 times. `segments`: never fall along a sequence.
All inputs are finite; a program needn't handle non-finite values.
Results may differ from a plain program's by a relative error of at most 0.039.
Values may be sent and summed in bfloat16 or wider, within the bound.
No kernel may reach another device: no remote copies, remote signals or barrier semaphores. Data moves between devices by JAX's collectives and lax.ppermute only.
A program may use at most 192 MiB of HBM per device.

v0:
```python
import math

import jax
import jax.numpy as jnp
from jax import lax
from jax.sharding import PartitionSpec as P

HEAD_DIM = 64
FF = 2048


EPSILON = 1e-05
MASKED = -1e30


def rotate(values, positions, direction):
    half_dim = values.shape[-1] // 2
    inverse = 10000.0 ** (-jnp.arange(half_dim, dtype=jnp.float32) / half_dim)
    angles = positions.astype(jnp.float32)[:, None] * inverse[None, :]
    cosine = jnp.cos(angles)[:, None, :]
    sine_part = jnp.sin(angles)[:, None, :]
    first_half = values[..., :half_dim]
    second = values[..., half_dim:]
    return jnp.concatenate(
        [
            first_half * cosine - direction * second * sine_part,
            second * cosine + direction * first_half * sine_part,
        ],
        axis=-1,
    )


def softmax_last(logits):
    shifted = jnp.exp(logits - jnp.max(logits, axis=-1, keepdims=True))
    return shifted / jnp.sum(shifted, axis=-1, keepdims=True)


def norm_scale(values):
    return lax.rsqrt(jnp.mean(values * values, axis=-1, keepdims=True) + EPSILON)


def norm_back(grad_in, values, factor, gain_vec):
    scaled = grad_in * gain_vec
    grad_gain = jnp.sum(grad_in * values * factor, axis=0)
    grad_values = factor * scaled - values * factor * factor * factor * jnp.mean(
        scaled * values, axis=-1, keepdims=True
    )
    return (grad_values, grad_gain)


def masked_scores(
    queries, key_rows, query_segments, key_segments, query_positions, key_positions, score_scale
):
    scores = (
        jnp.einsum("qhd,khd->hqk", queries, key_rows, preferred_element_type=jnp.float32)
        * score_scale
    )
    allowed = (query_segments[:, None] == key_segments[None, :]) & (
        key_positions[None, :] <= query_positions[:, None]
    )
    return (jnp.where(allowed[None], scores, MASKED), allowed)


def local(
    inputs,
    cotangent,
    qkv_weight,
    out_weight,
    norm_gains,
    route_weight,
    const_gate,
    const_vec,
    w_gate,
    w_up,
    w_down,
    prev_logits,
    routes,
    segments,
):
    micro_count = inputs.shape[0]
    row_count = inputs.shape[2]
    model_width = inputs.shape[3]
    head_count = model_width // HEAD_DIM
    score_scale = HEAD_DIM ** (-0.5)
    local_experts = w_gate.shape[0]
    experts = local_experts * lax.axis_size("experts")
    capacity = row_count * 5 // 16
    routed = prev_logits.shape[3]
    assigned = 2 * row_count
    head_shape = (row_count, head_count, HEAD_DIM)
    positions = lax.axis_index("context") * row_count + jnp.arange(row_count, dtype=jnp.int32)
    grad_qkv = jnp.zeros((3, model_width, model_width), jnp.float32)
    grad_out = jnp.zeros((model_width, model_width), jnp.float32)
    gain_first = jnp.zeros((model_width,), jnp.float32)
    gain_second = jnp.zeros((model_width,), jnp.float32)
    grad_vec = jnp.zeros((2, model_width), jnp.float32)
    grad_route = jnp.zeros((model_width, routed), jnp.float32)
    grad_mixer = jnp.zeros((model_width, 4), jnp.float32)
    grad_gate = jnp.zeros((local_experts, model_width, FF), jnp.float32)
    grad_up = jnp.zeros((local_experts, model_width, FF), jnp.float32)
    grad_down = jnp.zeros((local_experts, model_width, FF), jnp.float32)
    output_rows = []
    input_rows = []
    logit_rows = []
    for batch_index in range(micro_count):
        qkv_full, out_full, gains, vectors, route_full, mixer_full = (
            lax.all_gather(qkv_weight, ("context", "dp"), axis=1, tiled=True),
            lax.all_gather(out_weight, ("context", "dp"), axis=0, tiled=True),
            lax.all_gather(
                norm_gains.astype(jnp.bfloat16), ("context", "dp"), axis=1, tiled=True
            ).astype(norm_gains.dtype),
            lax.all_gather(
                const_vec.astype(jnp.bfloat16), ("context", "dp"), axis=1, tiled=True
            ).astype(const_vec.dtype),
            lax.all_gather(route_weight, ("context", "dp"), axis=0, tiled=True),
            lax.all_gather(const_gate, ("context", "dp"), axis=0, tiled=True),
        )
        gate_full, up_full, down_full = (
            lax.all_gather(w_gate, ("context", "dp"), axis=2, tiled=True),
            lax.all_gather(w_up, ("context", "dp"), axis=2, tiled=True),
            lax.all_gather(w_down, ("context", "dp"), axis=2, tiled=True),
        )
        token_rows = inputs[batch_index, 0].astype(jnp.float32)
        seg_rows = segments[batch_index, 0]
        route_rows = routes[batch_index, 0]
        grad_rows = cotangent[batch_index, 0].astype(jnp.float32)
        scale_first = norm_scale(token_rows)
        normed_in = (token_rows * scale_first * gains[0]).astype(jnp.bfloat16)
        projected = jnp.einsum(
            "qd,cde->cqe", normed_in, qkv_full, preferred_element_type=jnp.float32
        )
        queries = rotate(projected[0].reshape(head_shape), positions, 1.0).astype(jnp.bfloat16)
        rotated_keys = rotate(projected[1].reshape(head_shape), positions, 1.0).astype(jnp.bfloat16)
        values = projected[2].reshape(head_shape).astype(jnp.bfloat16)
        row_peak = jnp.full((head_count, row_count), MASKED, jnp.float32)
        key_block = lax.all_gather(rotated_keys, "context", axis=0, tiled=True)
        value_block = lax.all_gather(values, "context", axis=0, tiled=True)
        segment_block = lax.all_gather(seg_rows, "context", axis=0, tiled=True)
        key_positions = jnp.arange(key_block.shape[0], dtype=jnp.int32)
        scores, allowed = masked_scores(
            queries, key_block, seg_rows, segment_block, positions, key_positions, score_scale
        )
        new_peak = jnp.maximum(row_peak, jnp.max(scores, axis=-1))
        expo = jnp.where(allowed[None], jnp.exp(scores - new_peak[:, :, None]), 0.0)
        weighted = jnp.einsum(
            "hqk,khd->hqd",
            expo.astype(jnp.bfloat16),
            value_block,
            preferred_element_type=jnp.float32,
        )
        row_peak, row_total, weighted = (new_peak, jnp.sum(expo, axis=-1), weighted)
        log_total = row_peak + jnp.log(row_total)
        attn_heads = jnp.transpose(weighted / row_total[:, :, None], (1, 0, 2))
        attended = attn_heads.reshape(row_count, model_width).astype(jnp.bfloat16)
        hidden = token_rows + jnp.dot(attended, out_full, preferred_element_type=jnp.float32)
        scale_second = norm_scale(hidden)
        normed = hidden * scale_second * gains[1]
        normed_low = normed.astype(jnp.bfloat16)
        logits = (
            jnp.dot(normed_low, route_full, preferred_element_type=jnp.float32)
            + prev_logits[batch_index, 0]
        )
        probabilities = softmax_last(logits)
        gate_values = jnp.take_along_axis(probabilities, route_rows, axis=-1)
        route_ids = route_rows.reshape(-1)
        routed_ffn = route_ids < experts
        onehot = (route_ids[:, None] == jnp.arange(experts, dtype=jnp.int32)[None, :]).astype(
            jnp.int32
        )
        slot_index = jnp.sum((jnp.cumsum(onehot, axis=0) - onehot) * onehot, axis=-1)
        slot_table = (
            jnp.full((experts, capacity), assigned, jnp.int32)
            .at[jnp.where(routed_ffn, route_ids, experts), slot_index]
            .set(jnp.arange(assigned, dtype=jnp.int32), mode="drop")
        )
        token_of = jnp.where(slot_table < assigned, slot_table // 2, row_count)
        pad_rows = jnp.concatenate([normed_low, jnp.zeros((1, model_width), jnp.bfloat16)], axis=0)
        received = lax.all_to_all(
            pad_rows[token_of], "experts", split_axis=0, concat_axis=1, tiled=True
        )
        gate_act = jnp.einsum(
            "erd,edf->erf", received, gate_full, preferred_element_type=jnp.float32
        )
        up_act = jnp.einsum("erd,edf->erf", received, up_full, preferred_element_type=jnp.float32)
        sigma = jax.nn.sigmoid(gate_act)
        silu_act = gate_act * sigma
        inner_low = (silu_act * up_act).astype(jnp.bfloat16)
        expert_low = jnp.einsum(
            "erf,edf->erd", inner_low, down_full, preferred_element_type=jnp.float32
        ).astype(jnp.bfloat16)
        returned = lax.all_to_all(
            expert_low, "experts", split_axis=1, concat_axis=0, tiled=True
        ).reshape(experts * capacity, model_width)
        pick_index = jnp.where(routed_ffn, route_ids * capacity + slot_index, 0)
        expert_out = jnp.where(
            routed_ffn[:, None], returned[pick_index].astype(jnp.float32), 0.0
        ).reshape(row_count, 2, model_width)
        const_mix = softmax_last(
            jnp.dot(normed_low, mixer_full, preferred_element_type=jnp.float32).reshape(
                row_count, 2, 2
            )
        )
        const_out = (
            const_mix[:, :, 0:1] * normed[:, None, :] + const_mix[:, :, 1:2] * vectors[None, :, :]
        )
        copy_mask = (route_rows == experts + 1).astype(jnp.float32)
        const_pick = (
            route_rows[:, :, None] == experts + 2 + jnp.arange(2, dtype=jnp.int32)[None, None, :]
        ).astype(jnp.float32)
        branch = (
            expert_out
            + copy_mask[:, :, None] * normed[:, None, :]
            + jnp.einsum("qjc,qcd->qjd", const_pick, const_out, precision=lax.Precision.HIGHEST)
        )
        output_rows.append(
            (hidden + jnp.sum(gate_values[:, :, None] * branch, axis=1)).astype(jnp.bfloat16)
        )
        grad_branch = gate_values[:, :, None] * grad_rows[:, None, :]
        grad_gates = jnp.sum(grad_rows[:, None, :] * branch, axis=-1)
        grad_probs = jnp.sum(
            (route_rows[:, :, None] == jnp.arange(routed, dtype=jnp.int32)[None, None, :]).astype(
                jnp.float32
            )
            * grad_gates[:, :, None],
            axis=1,
        )
        grad_logits = probabilities * (
            grad_probs - jnp.sum(probabilities * grad_probs, axis=-1, keepdims=True)
        )
        logit_rows.append(grad_logits)
        normed_wide = normed_low.astype(jnp.float32)
        grad_route = grad_route + jnp.dot(
            normed_wide.T, grad_logits, precision=lax.Precision.HIGHEST
        )
        grad_normed = jnp.dot(
            grad_logits, route_full.astype(jnp.float32).T, precision=lax.Precision.HIGHEST
        )
        grad_normed = grad_normed + jnp.sum(copy_mask[:, :, None] * grad_branch, axis=1)
        grad_const = jnp.einsum(
            "qjc,qjd->qcd", const_pick, grad_branch, precision=lax.Precision.HIGHEST
        )
        grad_mix = jnp.stack(
            [
                jnp.sum(grad_const * normed[:, None, :], axis=-1),
                jnp.sum(grad_const * vectors[None, :, :], axis=-1),
            ],
            axis=-1,
        )
        grad_mix_logits = (
            const_mix * (grad_mix - jnp.sum(const_mix * grad_mix, axis=-1, keepdims=True))
        ).reshape(row_count, 4)
        grad_mixer = grad_mixer + jnp.dot(
            normed_wide.T, grad_mix_logits, precision=lax.Precision.HIGHEST
        )
        grad_normed = grad_normed + jnp.dot(
            grad_mix_logits, mixer_full.astype(jnp.float32).T, precision=lax.Precision.HIGHEST
        )
        grad_normed = grad_normed + jnp.sum(const_mix[:, :, 0:1] * grad_const, axis=1)
        grad_vec = grad_vec + jnp.sum(const_mix[:, :, 1:2] * grad_const, axis=0)
        grad_slots = jnp.where(
            routed_ffn[:, None], grad_branch.reshape(assigned, model_width), 0.0
        ).astype(jnp.bfloat16)
        grad_pad = jnp.concatenate([grad_slots, jnp.zeros((1, model_width), jnp.bfloat16)], axis=0)
        grad_received = lax.all_to_all(
            grad_pad[slot_table], "experts", split_axis=0, concat_axis=1, tiled=True
        )
        grad_inner = jnp.einsum(
            "erd,edf->erf", grad_received, down_full, preferred_element_type=jnp.float32
        )
        grad_down = grad_down + jnp.einsum(
            "erd,erf->edf", grad_received, inner_low, preferred_element_type=jnp.float32
        )
        grad_gate_low = (grad_inner * up_act * sigma * (1.0 + gate_act * (1.0 - sigma))).astype(
            jnp.bfloat16
        )
        grad_up_low = (grad_inner * silu_act).astype(jnp.bfloat16)
        grad_gate = grad_gate + jnp.einsum(
            "erd,erf->edf", received, grad_gate_low, preferred_element_type=jnp.float32
        )
        grad_up = grad_up + jnp.einsum(
            "erd,erf->edf", received, grad_up_low, preferred_element_type=jnp.float32
        )
        grad_entry = (
            jnp.einsum("erf,edf->erd", grad_gate_low, gate_full, preferred_element_type=jnp.float32)
            + jnp.einsum("erf,edf->erd", grad_up_low, up_full, preferred_element_type=jnp.float32)
        ).astype(jnp.bfloat16)
        grad_back = lax.all_to_all(
            grad_entry, "experts", split_axis=1, concat_axis=0, tiled=True
        ).reshape(experts * capacity, model_width)
        grad_normed = grad_normed + jnp.sum(
            jnp.where(routed_ffn[:, None], grad_back[pick_index].astype(jnp.float32), 0.0).reshape(
                row_count, 2, model_width
            ),
            axis=1,
        )
        grad_hidden_norm, gain_term = norm_back(grad_normed, hidden, scale_second, gains[1])
        gain_second = gain_second + gain_term
        grad_hidden = grad_rows + grad_hidden_norm
        grad_attn_low = grad_hidden.astype(jnp.bfloat16)
        grad_out = grad_out + jnp.dot(attended.T, grad_attn_low, preferred_element_type=jnp.float32)
        grad_attended = (
            jnp.dot(grad_attn_low, out_full.T, preferred_element_type=jnp.float32)
            .astype(jnp.bfloat16)
            .reshape(head_shape)
        )
        delta = jnp.sum(grad_attended.astype(jnp.float32) * attn_heads, axis=-1).T
        zero_heads = jnp.zeros(head_shape, jnp.float32)
        key_all, value_all, segment_all = (
            lax.all_gather(rotated_keys, "context", axis=0, tiled=True),
            lax.all_gather(values, "context", axis=0, tiled=True),
            lax.all_gather(seg_rows, "context", axis=0, tiled=True),
        )
        total_keys = key_all.shape[0]
        group_count = math.gcd(total_keys // row_count, max(1, 512 // row_count))
        block_rows = row_count * group_count
        block_count = total_keys // block_rows

        def back_block(grad_query, block_parts):
            key_block, value_block, segment_block, block_start = block_parts
            key_positions = block_start + jnp.arange(block_rows, dtype=jnp.int32)
            scores, allowed = masked_scores(
                queries, key_block, seg_rows, segment_block, positions, key_positions, score_scale
            )
            probability = jnp.where(allowed[None], jnp.exp(scores - log_total[:, :, None]), 0.0)
            grad_prob = jnp.einsum(
                "qhd,khd->hqk", grad_attended, value_block, preferred_element_type=jnp.float32
            )
            grad_score = (probability * (grad_prob - delta[:, :, None])).astype(jnp.bfloat16)
            grad_query = (
                grad_query
                + jnp.einsum(
                    "hqk,khd->qhd", grad_score, key_block, preferred_element_type=jnp.float32
                )
                * score_scale
            )
            grad_key = (
                jnp.einsum("hqk,qhd->khd", grad_score, queries, preferred_element_type=jnp.float32)
                * score_scale
            )
            grad_value = jnp.einsum(
                "hqk,qhd->khd",
                probability.astype(jnp.bfloat16),
                grad_attended,
                preferred_element_type=jnp.float32,
            )
            return (grad_query, (grad_key, grad_value))

        block_starts = jnp.arange(block_count, dtype=jnp.int32) * block_rows
        grad_query, (key_terms, value_terms) = lax.scan(
            back_block,
            zero_heads,
            (
                key_all.reshape(block_count, block_rows, head_count, HEAD_DIM),
                value_all.reshape(block_count, block_rows, head_count, HEAD_DIM),
                segment_all.reshape(block_count, block_rows),
                block_starts,
            ),
        )
        grad_key, grad_value = (
            lax.psum_scatter(
                key_terms.reshape(total_keys, head_count, HEAD_DIM).astype(jnp.bfloat16),
                "context",
                scatter_dimension=0,
                tiled=True,
            ).astype(jnp.float32),
            lax.psum_scatter(
                value_terms.reshape(total_keys, head_count, HEAD_DIM).astype(jnp.bfloat16),
                "context",
                scatter_dimension=0,
                tiled=True,
            ).astype(jnp.float32),
        )
        grad_projected = jnp.stack(
            [
                rotate(grad_query, positions, -1.0).reshape(row_count, model_width),
                rotate(grad_key, positions, -1.0).reshape(row_count, model_width),
                grad_value.reshape(row_count, model_width),
            ]
        ).astype(jnp.bfloat16)
        grad_qkv = grad_qkv + jnp.einsum(
            "qd,cqe->cde", normed_in, grad_projected, preferred_element_type=jnp.float32
        )
        grad_normed_in = jnp.einsum(
            "cqe,cde->qd", grad_projected, qkv_full, preferred_element_type=jnp.float32
        )
        grad_token_norm, gain_term = norm_back(grad_normed_in, token_rows, scale_first, gains[0])
        gain_first = gain_first + gain_term
        input_rows.append(grad_hidden + grad_token_norm)
    grad_gain = jnp.stack([gain_first, gain_second])
    (
        grad_qkv,
        grad_out,
        grad_gain,
        grad_vec,
        grad_route,
        grad_mixer,
        grad_gate,
        grad_up,
        grad_down,
    ) = (
        lax.psum_scatter(
            grad_qkv.astype(jnp.bfloat16), ("context", "dp"), scatter_dimension=1, tiled=True
        ).astype(jnp.float32),
        lax.psum_scatter(
            grad_out.astype(jnp.bfloat16), ("context", "dp"), scatter_dimension=0, tiled=True
        ).astype(jnp.float32),
        lax.psum_scatter(
            grad_gain.astype(jnp.bfloat16), ("context", "dp"), scatter_dimension=1, tiled=True
        ).astype(jnp.float32),
        lax.psum_scatter(
            grad_vec.astype(jnp.bfloat16), ("context", "dp"), scatter_dimension=1, tiled=True
        ).astype(jnp.float32),
        lax.psum_scatter(
            grad_route.astype(jnp.bfloat16), ("context", "dp"), scatter_dimension=0, tiled=True
        ).astype(jnp.float32),
        lax.psum_scatter(
            grad_mixer.astype(jnp.bfloat16), ("context", "dp"), scatter_dimension=0, tiled=True
        ).astype(jnp.float32),
        lax.psum_scatter(
            grad_gate.astype(jnp.bfloat16), ("context", "dp"), scatter_dimension=2, tiled=True
        ).astype(jnp.float32),
        lax.psum_scatter(
            grad_up.astype(jnp.bfloat16), ("context", "dp"), scatter_dimension=2, tiled=True
        ).astype(jnp.float32),
        lax.psum_scatter(
            grad_down.astype(jnp.bfloat16), ("context", "dp"), scatter_dimension=2, tiled=True
        ).astype(jnp.float32),
    )
    grad_qkv, grad_out, grad_gain, grad_vec, grad_route, grad_mixer = (
        lax.psum(grad_qkv.astype(jnp.bfloat16), "experts").astype(jnp.float32),
        lax.psum(grad_out.astype(jnp.bfloat16), "experts").astype(jnp.float32),
        lax.psum(grad_gain.astype(jnp.bfloat16), "experts").astype(jnp.float32),
        lax.psum(grad_vec.astype(jnp.bfloat16), "experts").astype(jnp.float32),
        lax.psum(grad_route.astype(jnp.bfloat16), "experts").astype(jnp.float32),
        lax.psum(grad_mixer.astype(jnp.bfloat16), "experts").astype(jnp.float32),
    )
    output = jnp.stack(output_rows)[:, None]
    input_grad = jnp.stack(input_rows)[:, None]
    logit_grad = jnp.stack(logit_rows)[:, None]
    return (
        output,
        input_grad,
        logit_grad,
        grad_qkv,
        grad_out,
        grad_gain,
        grad_route,
        grad_mixer,
        grad_vec,
        grad_gate,
        grad_up,
        grad_down,
    )


def solution(mesh):
    in_specs = (
        P(None, ("experts", "dp"), "context", None),
        P(None, ("experts", "dp"), "context", None),
        P(None, ("context", "dp"), None),
        P(("context", "dp"), None),
        P(None, ("context", "dp")),
        P(("context", "dp"), None),
        P(("context", "dp"), None),
        P(None, ("context", "dp")),
        P("experts", None, ("context", "dp")),
        P("experts", None, ("context", "dp")),
        P("experts", None, ("context", "dp")),
        P(None, ("experts", "dp"), "context", None),
        P(None, ("experts", "dp"), "context", None),
        P(None, ("experts", "dp"), "context"),
    )
    out_specs = (
        P(None, ("experts", "dp"), "context", None),
        P(None, ("experts", "dp"), "context", None),
        P(None, ("experts", "dp"), "context", None),
        P(None, ("context", "dp"), None),
        P(("context", "dp"), None),
        P(None, ("context", "dp")),
        P(("context", "dp"), None),
        P(("context", "dp"), None),
        P(None, ("context", "dp")),
        P("experts", None, ("context", "dp")),
        P("experts", None, ("context", "dp")),
        P("experts", None, ("context", "dp")),
    )
    return jax.shard_map(local, mesh=mesh, in_specs=in_specs, out_specs=out_specs, check_vma=False)
```

profile of v0, /device:TPU:0, one launch (start us, length us, event | category | flops | bytes accessed | tf_op | source)
XLA Modules:
  0.0 1102.4 jit_solution(15480286832784686450)
XLA Ops:
  8.6 13.4 %all-gather.2 = bf16[8,96,2]{1,2,0:T(2,128)(2,1)S(1)} all-gather(bf16[1,96,2]{1,2,0:T(2,128)(2,1)S(1)} %convert_bitcast_fusion.5), channel_id=1, replica_groups=mesh['experts'=4,'context'=4,'dp'=2] {'context','dp'}, dimensions={0}, use_global_device_ids=true | all-gather | bytes 3456 | tf_op jit(solution)/shard_map/all_gather | solution.py:109
  24.4 29.5 %all-gather.16.cloned.1.call-done = bf16[3,768,768]{2,1,0:T(8,128)(2,1)} async-done(((bf16[3,96,768]{2,1,0:T(8,128)(2,1)}), bf16[3,768,768]{2,1,0:T(8,128)(2,1)}) %all-gather.16.cloned.1.call-update) | async-done | bytes 3538960 | tf_op jit(solution)/shard_map/all_gather | solution.py:107
  107.2 13.5 %all-gather.3 = bf16[8,96,8]{1,2,0:T(8,128)(2,1)S(1)} all-gather(bf16[1,96,8]{1,2,0:T(8,128)(2,1)S(1)} %bitcast.709), channel_id=1, replica_groups=mesh['experts'=4,'context'=4,'dp'=2] {'context','dp'}, dimensions={0}, use_global_device_ids=true | all-gather | bytes 13824 | tf_op jit(solution)/shard_map/all_gather | solution.py:115
  123.7 22.5 %scatter_fusion.1 = s32[4,80]{1,0:T(4,128)S(1)} fusion(s32[4,80]{1,0:T(4,128)S(1)} %broadcast.652.clone, s32[512]{0:T(512)S(1)} %bitcast.607, s32[512]{0:T(512)S(1)} %iota.85), kind=kCustom, calls=%fused_computation.11 | custom fusion | bytes 10240 | tf_op jit(solution)/shard_map/scatter | solution.py:174
  156.4 10.1 all-gather.5
  173.6 22.5 %scatter_fusion = s32[4,80]{1,0:T(4,128)S(1)} fusion(s32[4,80]{1,0:T(4,128)S(1)} %broadcast.652.clone.1, s32[512]{0:T(512)S(1)} %bitcast.606, s32[512]{0:T(512)S(1)} %iota.83), kind=kCustom, calls=%fused_computation.10 | custom fusion | bytes 10240 | tf_op jit(solution)/shard_map/scatter | solution.py:174
  282.8 14.5 %multiply_reduce_fusion.1 = (f32[2,768]{1,0:T(2,128)}, f32[256,768]{1,0:T(8,128)}, f32[256,2]{1,0:T(8,128)S(1)}, f32[256,2]{1,0:T(8,128)S(1)}, f32[256,2]{1,0:T(...) fusion(f32[256,2]{1,0:T(8,128)S(1)} %bitcast.675, f32[256,2]{1,0:T(8,128)S(1)} %bitcast.677, ...), kind=kOutput, calls=%fused_computation.159 | convolution fusion | flops 15724544 | bytes 5543944 | tf_op jit(solution)/shard_map/qjc,qjd->qcd/dot_general | solution.py:239
  340.2 25.8 %all-gather.24.cloned.1.call-done = bf16[1,768,2048]{2,1,0:T(8,128)(2,1)} async-done(((bf16[1,768,256]{2,1,0:T(8,128)(2,1)}), bf16[1,768,2048]{2,1,0:T(8,128)(2,1)}) %all-gather.24.cloned.1.call-update) | async-done | bytes 3145744 | tf_op jit(solution)/shard_map/all_gather | solution.py:119
  451.3 13.7 %multiply_reduce_fusion.5 = (f32[256,2]{1,0:T(8,128)S(1)}, f32[256,768]{1,0:T(8,128)}, f32[256,768]{1,0:T(8,128)}) fusion(f32[256,768]{1,0:T(8,128)S(1)} %copy-done.69, f32[256,2]{1,0:T(8,128)} %copy-done.109, f32[256,2]{1,0:T(8,128)} %get-tuple-element.713, f32[256,2]{1,0:T(8,128)} %bitcast.682, f32[256,2]{1,0:T(8,128)} %bitcast.680, ...), kind=kOutput, calls=%fused_computation.167 | convolution fusion | flops 14549504 | bytes 4737544 | tf_op jit(solution)/shard_map/qjc,qcd->qjd/dot_general | solution.py:213
  496.9 13.8 %multiply_reduce_fusion.9 = (f32[256,2]{1,0:T(8,128)}, f32[256,768]{1,0:T(8,128)S(1)}, f32[256,768]{1,0:T(8,128)}) fusion(f32[256,768]{1,0:T(8,128)S(1)} %copy-done.66, f32[256,2]{1,0:T(8,128)S(1)} %copy-done.108, f32[256,2]{1,0:T(8,128)} %get-tuple-element.711, f32[2,768]{1,0:T(2,128)S(1)} %bitcast.708, f32[256,2]{1,0:T(8,128)} %bitcast.676, ...), kind=kOutput, calls=%fused_computation.175 | convolution fusion | flops 14549504 | bytes 4737544 | tf_op jit(solution)/shard_map/qjc,qcd->qjd/dot_general | solution.py:213
  525.0 32.7 %while.31 = (s32[]{:T(128)}, f32[256,12,64]{0,2,1:T(8,128)}, bf16[2,512,12,64]{1,3,2,0:T(8,128)(2,1)}, bf16[2,512,12,64]{1,3,2,0:T(8,128)(2,1)}, bf16[2,512,12,6...) while((s32[]{:T(128)}, f32[256,12,64]{0,2,1:T(8,128)}, ...), condition=%wide.region_54.56_spmd.clone, body=%wide.region_53.55_spmd.clone.sunk | while | flops 1026884352 | bytes 123553488 | solution.py:349
  566.0 36.4 %while.30 = (s32[]{:T(128)}, f32[256,12,64]{0,2,1:T(8,128)}, bf16[2,512,12,64]{1,3,2,0:T(8,128)(2,1)}, bf16[2,512,12,64]{1,3,2,0:T(8,128)(2,1)}, bf16[2,512,12,6...) while((s32[]{:T(128)}, f32[256,12,64]{0,2,1:T(8,128)}, ...), condition=%wide.region_38.40_spmd.clone, body=%wide.region_37.39_spmd.clone.sunk | while | flops 1026884352 | bytes 110970456 | solution.py:349
  615.2 25.4 %reduce-scatter.24.cloned.1.call-done = bf16[256,12,64]{0,2,1:T(8,128)(2,1)} async-done(((bf16[1024,12,64]{0,2,1:T(8,128)(2,1)}), bf16[256,12,64]{0,2,1:T(8,128)(2,1)}) %reduce-scatter.24.cloned.1.call-update) | async-done | bytes 393232 | tf_op jit(solution)/shard_map/reduce_scatter | solution.py:360
  641.6 36.0 %reduce-scatter.28.cloned.1.call-done = bf16[256,12,64]{0,2,1:T(8,128)(2,1)} async-done(((bf16[1024,12,64]{0,2,1:T(8,128)(2,1)}), bf16[256,12,64]{0,2,1:T(8,128)(2,1)}) %reduce-scatter.28.cloned.1.call-update) | async-done | bytes 393232 | tf_op jit(solution)/shard_map/reduce_scatter | solution.py:360
  681.8 32.3 %reduce-scatter.26.cloned.1.call-done = bf16[256,12,64]{0,2,1:T(8,128)(2,1)} async-done(((bf16[1024,12,64]{0,2,1:T(8,128)(2,1)}), bf16[256,12,64]{0,2,1:T(8,128)(2,1)}) %reduce-scatter.26.cloned.1.call-update) | async-done | bytes 393232 | tf_op jit(solution)/shard_map/reduce_scatter | solution.py:366
  778.5 28.2 %reduce-scatter.44.cloned.1.call-done = bf16[96,8]{1,0:T(8,128)(2,1)} async-done(((bf16[768,8]{1,0:T(8,128)(2,1)}), bf16[96,8]{1,0:T(8,128)(2,1)}) %reduce-scatter.44.cloned.1.call-update) | async-done | bytes 1552
  807.5 43.5 %reduce-scatter.40.cloned.1.call-done = bf16[96,2304]{1,0:T(8,128)(2,1)} async-done(((bf16[768,2304]{1,0:T(8,128)(2,1)}), bf16[96,2304]{1,0:T(8,128)(2,1)}) %reduce-scatter.40.cloned.1.call-update) | async-done | bytes 442384
  853.8 31.1 %reduce-scatter.32.cloned.1.call-done = bf16[96,768]{1,0:T(8,128)(2,1)} async-done(((bf16[768,768]{1,0:T(8,128)(2,1)}), bf16[96,768]{1,0:T(8,128)(2,1)}) %reduce-scatter.32.cloned.1.call-update) | async-done | bytes 147472 | tf_op jit(solution)/shard_map/reduce_scatter | solution.py:404
  888.1 28.2 %reduce-scatter.42.cloned.1.call-done = bf16[96,2]{1,0:T(8,128)(2,1)} async-done(((bf16[768,2]{1,0:T(8,128)(2,1)}), bf16[96,2]{1,0:T(8,128)(2,1)}) %reduce-scatter.42.cloned.1.call-update) | async-done | bytes 400
  917.1 9.9 all-reduce.4
  929.3 27.8 %reduce-scatter.34.cloned.1.call-done = bf16[1,768,256]{2,1,0:T(8,128)(2,1)} async-done(((bf16[1,768,2048]{2,1,0:T(8,128)(2,1)}), bf16[1,768,256]{2,1,0:T(8,128)(2,1)}) %reduce-scatter.34.cloned.1.call-update) | async-done | bytes 393232 | tf_op jit(solution)/shard_map/reduce_scatter | solution.py:419
  959.0 40.0 %reduce-scatter.36.cloned.1.call-done = bf16[1,768,256]{2,1,0:T(8,128)(2,1)} async-done(((bf16[1,768,2048]{2,1,0:T(8,128)(2,1)}), bf16[1,768,256]{2,1,0:T(8,128)(2,1)}) %reduce-scatter.36.cloned.1.call-update) | async-done | bytes 393232 | tf_op jit(solution)/shard_map/reduce_scatter | solution.py:422
  1000.9 39.9 %reduce-scatter.38.cloned.1.call-done = bf16[1,768,256]{2,1,0:T(8,128)(2,1)} async-done(((bf16[1,768,2048]{2,1,0:T(8,128)(2,1)}), bf16[1,768,256]{2,1,0:T(8,128)(2,1)}) %reduce-scatter.38.cloned.1.call-update) | async-done | bytes 393232 | tf_op jit(solution)/shard_map/reduce_scatter | solution.py:425
  1042.8 49.0 %all-reduce.8.cloned.1.call-done = (bf16[3,96,768]{1,2,0:T(8,128)(2,1)}, bf16[96,768]{1,0:T(8,128)(2,1)}) async-done(((bf16[3,96,768]{1,2,0:T(8,128)(2,1)}, bf16[96,768]{1,0:T(8,128)(2,1)}), (bf16[3,96,768]{1,2,0:T(8,128)(2,1)}, bf16[96,768]{1,0:T(8,128)(2,1)})) %all-reduce.8.cloned.1.call-update) | async-done | bytes 589840 | tf_op jit(solution)/shard_map/psum | solution.py:430
  (894 shorter events, 514.0 us)
Async XLA Ops:
  7.9 196.0 %all-gather.18.cloned.1.call-start = ((), (), s32[]{:S(2)}) async-start(), calls=%async_computation.22 | async-start | bytes 1966080 | tf_op jit(solution)/shard_map/all_gather | solution.py:136
  74.0 142.7 %all-gather.20.cloned.1.call-start = ((), (), s32[]{:S(2)}) async-start(), calls=%async_computation.23 | async-start | bytes 1966080 | tf_op jit(solution)/shard_map/all_gather | solution.py:137
  76.2 148.5 %all-gather.22.cloned.1.call-start = ((), (), s32[]{:S(2)}) async-start(), calls=%async_computation.24 | async-start | bytes 1327104 | tf_op jit(solution)/shard_map/all_gather | solution.py:108
  76.8 150.0 %all-gather.30.cloned.1.call-start = ((), (), s32[]{:S(2)}) async-start(), calls=%async_computation.28 | async-start | bytes 1966080 | tf_op jit(solution)/shard_map/all_gather | solution.py:136
  77.6 171.2 %all-gather.32.cloned.1.call-start = ((), (), s32[]{:S(2)}) async-start(), calls=%async_computation.29 | async-start | bytes 1966080 | tf_op jit(solution)/shard_map/all_gather | solution.py:137
  79.8 244.5 %all-gather.28.cloned.1.call-start = ((), (), s32[]{:S(2)}) async-start(), calls=%async_computation.27 | async-start | bytes 3538944 | tf_op jit(solution)/shard_map/all_gather | solution.py:121
  80.6 255.0 %all-gather.26.cloned.1.call-start = ((), (), s32[]{:S(2)}) async-start(), calls=%async_computation.26 | async-start | bytes 3538944 | tf_op jit(solution)/shard_map/all_gather | solution.py:120
  81.3 284.7 %all-gather.24.cloned.1.call-start = ((), (), s32[]{:S(2)}) async-start(), calls=%async_computation.25 | async-start | bytes 3538944 | tf_op jit(solution)/shard_map/all_gather | solution.py:119
  267.2 52.8 %all-to-all-start.6 = ((bf16[4,80,768]{2,1,0:T(8,128)(2,1)}), bf16[4,80,768]{2,1,0:T(8,128)(2,1)}, u32[]{:S(2)}, u32[]{:S(2)}) async-start(bf16[4,80,768]{2,1,0:T(8,128)(2,1)} %bitcast.81), calls=%async_computation.8 | async-start | bytes 983040 | tf_op jit(solution)/shard_map/all_to_all | solution.py:264
  331.6 63.9 %all-to-all-start.4 = ((bf16[4,80,768]{2,1,0:T(8,128)(2,1)}), bf16[4,80,768]{2,1,0:T(8,128)(2,1)S(1)}, u32[]{:S(2)}, u32[]{:S(2)}) async-start(bf16[4,80,768]{2,1,0:T(8,128)(2,1)} %bitcast.67), calls=%async_computation.4 | async-start | bytes 983040 | tf_op jit(solution)/shard_map/all_to_all | solution.py:264
  469.4 143.8 %reduce-scatter.30.cloned.1.call-start = ((), (), s32[]{:S(2)}) async-start(), calls=%async_computation.33 | async-start | bytes 1966080 | tf_op jit(solution)/shard_map/reduce_scatter | solution.py:366
  560.6 79.9 %reduce-scatter.24.cloned.1.call-start = ((), (), s32[]{:S(2)}) async-start(), calls=%async_computation.30 | async-start | bytes 1966080 | tf_op jit(solution)/shard_map/reduce_scatter | solution.py:360
  605.3 72.2 %reduce-scatter.28.cloned.1.call-start = ((), (), s32[]{:S(2)}) async-start(), calls=%async_computation.32 | async-start | bytes 1966080 | tf_op jit(solution)/shard_map/reduce_scatter | solution.py:360
  606.8 107.4 %reduce-scatter.26.cloned.1.call-start = ((), (), s32[]{:S(2)}) async-start(), calls=%async_computation.31 | async-start | bytes 1966080 | tf_op jit(solution)/shard_map/reduce_scatter | solution.py:366
  608.8 159.1 %reduce-scatter.48.cloned.1.call-start = ((), (), s32[]{:S(2)}) async-start(), calls=%async_computation.42 | async-start | bytes 221184
  610.5 165.7 %reduce-scatter.46.cloned.1.call-start = ((), (), s32[]{:S(2)}) async-start(), calls=%async_computation.41 | async-start | bytes 221184
  611.7 195.0 %reduce-scatter.44.cloned.1.call-start = ((), (), s32[]{:S(2)}) async-start(), calls=%async_computation.40 | async-start | bytes 221184
  613.2 237.8 %reduce-scatter.40.cloned.1.call-start = ((), (), s32[]{:S(2)}) async-start(), calls=%async_computation.38 | async-start | bytes 3981312
  730.5 154.4 %reduce-scatter.32.cloned.1.call-start = ((), (), s32[]{:S(2)}) async-start(), calls=%async_computation.34 | async-start | bytes 1327104 | tf_op jit(solution)/shard_map/reduce_scatter | solution.py:404
  733.7 182.6 %reduce-scatter.42.cloned.1.call-start = ((), (), s32[]{:S(2)}) async-start(), calls=%async_computation.39 | async-start | bytes 221184
  745.1 212.0 %reduce-scatter.34.cloned.1.call-start = ((), (), s32[]{:S(2)}) async-start(), calls=%async_computation.35 | async-start | bytes 3538944 | tf_op jit(solution)/shard_map/reduce_scatter | solution.py:419
  752.3 246.7 %reduce-scatter.36.cloned.1.call-start = ((), (), s32[]{:S(2)}) async-start(), calls=%async_computation.36 | async-start | bytes 3538944 | tf_op jit(solution)/shard_map/reduce_scatter | solution.py:422
  760.0 280.9 %reduce-scatter.38.cloned.1.call-start = ((), (), s32[]{:S(2)}) async-start(), calls=%async_computation.37 | async-start | bytes 3538944 | tf_op jit(solution)/shard_map/reduce_scatter | solution.py:425
  767.9 324.0 %all-reduce.8.cloned.1.call-start = ((), (), s32[]{:S(2)}) async-start(), calls=%async_computation.43 | async-start | bytes 1474560 | tf_op jit(solution)/shard_map/psum | solution.py:430
  (240 other events, 3704.2 us)
Sparse Core Ops, SparseCore 0:
  9.6 44.2 all-gather.15
  74.2 36.7 all-gather.17
  113.1 35.9 all-gather.19
  150.5 20.8 all-gather.21
  173.4 37.3 all-gather.29
  212.9 35.9 all-gather.31
  250.4 37.4 all-gather.27
  289.5 37.4 all-gather.25
  328.6 37.4 all-gather.23
  560.7 35.0 reduce-scatter.29
  605.4 35.0 reduce-scatter.23
  643.2 34.2 reduce-scatter.27
  679.8 34.2 reduce-scatter.25
  716.2 29.2 reduce-scatter.47
  747.7 28.4 reduce-scatter.45
  778.2 28.4 reduce-scatter.43
  809.0 41.9 reduce-scatter.39
  853.7 31.1 reduce-scatter.31
  887.7 28.5 reduce-scatter.41
  918.6 38.4 reduce-scatter.33
  959.5 39.4 reduce-scatter.35
  1001.4 39.4 reduce-scatter.37
  1044.3 47.4 all-reduce.7
where the time goes:
time: 1110 us; the launch traced here: 1100 us
  waiting for transfers between devices  463 us (42%)
  local copies, waits for them, and re-layouts  217 us (20%)
  matrix products  212 us (19%)
  other arithmetic  86.7 us (8%)
  blocking collectives  72.7 us (7%)
  starting transfers between devices  33.8 us (3%)
  between operations  17 us (2%)
    unnamed x28, waiting for transfers between devices  111 us
    reduce_scatter x2, waiting for transfers between devices, local(): lax.psum_scatter(key_terms.reshape(total_keys, head_count, HEAD_DIM).asty...  61.3 us
    unnamed x380, local copies, waits for them, and re-layouts  57.7 us
    psum x1, waiting for transfers between devices, local(): lax.psum(grad_qkv.astype(jnp.bfloat16), 'experts').astype(jnp.float32)  49 us
    scatter x2, local copies, waits for them, and re-layouts, local(): slot_table = jnp.full((experts, capacity), assigned, jnp.int32).at[jnp.wh...  45 us
    reduce_scatter x1, waiting for transfers between devices, local(): lax.psum_scatter(grad_up.astype(jnp.bfloat16), ('context', 'dp'), scatter...  40 us
    reduce_scatter x1, waiting for transfers between devices, local(): lax.psum_scatter(grad_down.astype(jnp.bfloat16), ('context', 'dp'), scatt...  39.9 us
    reduce_scatter x2, waiting for transfers between devices, local(): lax.psum_scatter(value_terms.reshape(total_keys, head_count, HEAD_DIM).as...  32.3 us
  transfers between devices with their start and end apart: 31, of which 17 were waited for; matrix products, arithmetic and copies ran while one was open for 36% of the time, Pallas kernels for 0%

commit v1 on v0

--- a/solution.py
+++ b/solution.py
@@ -1,8 +1,12 @@
+import functools
 import math
 
 import jax
 import jax.numpy as jnp
+import numpy as np
 from jax import lax
+from jax.experimental import pallas as pl
+from jax.experimental.pallas import tpu as pltpu
 from jax.sharding import PartitionSpec as P
 
 HEAD_DIM = 64
@@ -61,7 +65,7 @@
     return (jnp.where(allowed[None], scores, MASKED), allowed)
 
 
-def local(
+def general_local(
     inputs,
     cotangent,
     qkv_weight,
@@ -453,7 +457,924 @@
     )
 
 
+BF = jnp.bfloat16
+F32 = jnp.float32
+BLOCK = 256
+RING = 4
+PIECES = tuple((k, own) for k in range(RING) for own in (True, False))
+VMEM_BYTES = 60 * 2**20
+
+
+def dot(left, right, left_dim, right_dim):
+    return lax.dot_general(
+        left, right, (((left_dim,), (right_dim,)), ((), ())), preferred_element_type=F32
+    )
+
+
+def iota(shape, dim):
+    return lax.broadcasted_iota(jnp.int32, shape, dim)
+
+
+def split3(values):
+    high = values.astype(BF).astype(F32)
+    rest = values - high
+    middle = rest.astype(BF).astype(F32)
+    return (high, middle, rest - middle)
+
+
+def split2(values):
+    high = values.astype(BF)
+    return (high, (values - high.astype(F32)).astype(BF))
+
+
+def rows_of(parts, count):
+    width = parts[0].shape[1]
+    index = iota((count, width), 0)
+    total = jnp.zeros((count, width), F32)
+    for place, part in enumerate(parts):
+        total = jnp.where(index == place, jnp.broadcast_to(part, (count, width)), total)
+    return total
+
+
+def column_of(row, width=128):
+    stacked = rows_of(split3(row), 16).astype(BF)
+    return dot(stacked, jnp.ones((16, width), BF), 0, 0)
+
+
+def wide(column, copies):
+    return jnp.concatenate([column] * copies, axis=1)
+
+
+def kernel_call(body, idx, args, outs, flops, grid=None, in_specs=None, out_specs=None, scratch=()):
+    moved = sum(a.size * a.dtype.itemsize for a in args)
+    moved += sum(math.prod(s) * jnp.dtype(d).itemsize for s, d in outs)
+    whole = pl.BlockSpec(memory_space=pltpu.VMEM)
+    extra = {} if grid is None else {"grid": grid}
+    return pl.pallas_call(
+        body,
+        out_shape=[jax.ShapeDtypeStruct(s, d) for s, d in outs],
+        in_specs=[pl.BlockSpec(memory_space=pltpu.SMEM)]
+        + (in_specs if in_specs is not None else [whole] * len(args)),
+        out_specs=out_specs if out_specs is not None else [whole] * len(outs),
+        scratch_shapes=list(scratch),
+        compiler_params=pltpu.CompilerParams(vmem_limit_bytes=VMEM_BYTES),
+        cost_estimate=pl.CostEstimate(flops=flops, bytes_accessed=moved, transcendentals=0),
+        **extra,
+    )(idx, *args)
+
+
+def rope_tables(length):
+    half = HEAD_DIM // 2
+    inverse = (10000.0 ** (-np.arange(half, dtype=np.float32) / half)).astype(np.float32)
+    angles = (np.arange(length, dtype=np.float32)[:, None] * inverse[None, :]).astype(np.float64)
+    cosine, sine = np.cos(angles), np.sin(angles)
+    cosine = np.concatenate([cosine] * 4, axis=1).astype(np.float32)
+    sine = np.concatenate([-sine, sine] * 2, axis=1).astype(np.float32)
+    return cosine, sine
+
+
+def turn(values, cosine, sine, direction):
+    width = values.shape[1]
+    copies = width // cosine.shape[1]
+    ahead = pltpu.roll(values, width - HEAD_DIM // 2, 1)
+    behind = pltpu.roll(values, HEAD_DIM // 2, 1)
+    first = (iota(values.shape, 1) & (HEAD_DIM - 1)) < HEAD_DIM // 2
+    partner = jnp.where(first, ahead, behind)
+    return values * wide(cosine, copies) + direction * (partner * wide(sine, copies))
+
+
+def project_kernel(idx, xa, xb, ya, yb, params, cosine, sine, *refs):
+    pieces, (q_ref, k_ref, v_ref, normed_ref, x_ref, w_ref) = refs[:8], refs[8:]
+    z, core, flip = idx[1], idx[2], idx[3]
+    depth, width = pieces[0].shape[1], pieces[0].shape[2]
+    for (k, own), piece in zip(PIECES, pieces):
+        shard = lax.rem(z + k, RING) * 2 + (core if own else 1 - core)
+        rows = pl.ds(pl.multiple_of(shard * depth, 16), depth)
+        for j in range(3):
+            w_ref[rows, j * width : (j + 1) * width] = piece[j]
+    for ref, half, slot in ((xa, core, 0), (xb, core, 1), (ya, 1 - core, 0), (yb, 1 - core, 1)):
+        block = 2 * half + (flip if slot == 0 else 1 - flip)
+        x_ref[pl.ds(pl.multiple_of(block * BLOCK, BLOCK), BLOCK), :] = ref[...]
+    gain = params[14:15, :]
+
+    def step(i, carry):
+        rows = pl.ds(pl.multiple_of(i * BLOCK, BLOCK), BLOCK)
+        x = x_ref[rows, :].astype(F32)
+        normed = (x * norm_scale(x) * gain).astype(BF)
+        normed_ref[rows, :] = normed
+        cos_rows, sin_rows = cosine[rows, :], sine[rows, :]
+        queries = turn(dot(normed, w_ref[:, :width], 1, 0), cos_rows, sin_rows, 1.0)
+        q_ref[rows, :] = (queries * HEAD_DIM**-0.5).astype(BF)
+        keys = turn(dot(normed, w_ref[:, width : 2 * width], 1, 0), cos_rows, sin_rows, 1.0)
+        k_ref[rows, :] = keys.astype(BF)
+        v_ref[rows, :] = dot(normed, w_ref[:, 2 * width :], 1, 0).astype(BF)
+        return carry
+
+    lax.fori_loop(0, x_ref.shape[0] // BLOCK, step, 0)
+
+
+def mask_of(seg_row, seg_col, i):
+    n = (i + 1) * BLOCK
+    mine = seg_row[:1, i * BLOCK : n]
+    key_index, query_index = iota((BLOCK, BLOCK), 0), iota((BLOCK, BLOCK), 1)
+    last = (seg_col[i * BLOCK : n, :1] == mine) & (key_index <= query_index)
+    bias = jnp.where(last, 0.0, MASKED)
+    if i > 0:
+        before = jnp.where(seg_col[: i * BLOCK, :1] == mine, 0.0, MASKED)
+        bias = jnp.concatenate([before, bias], axis=0)
+    return bias
+
+
+def attend_kernel(idx, q_ref, k_ref, v_ref, seg_row, seg_col, keep_ref, send_ref, lse_ref):
+    core, flip = idx[2], idx[3]
+    low_lanes = iota((BLOCK, 2 * HEAD_DIM), 1) < HEAD_DIM
+    for i in range(q_ref.shape[0] // BLOCK):
+        n = (i + 1) * BLOCK
+        queries = q_ref[i * BLOCK : n, :]
+        keys, values = k_ref[:n, :], v_ref[:n, :]
+        bias = mask_of(seg_row, seg_col, i)
+        outs = []
+        for head in range(2):
+            mine = low_lanes if head == 0 else ~low_lanes
+            scores = dot(keys, jnp.where(mine, queries, 0), 1, 1) + bias
+            peak = jnp.max(scores, axis=0, keepdims=True)
+            weights = jnp.exp(scores - peak)
+            total = jnp.sum(weights, axis=0, keepdims=True)
+            out = dot(values, weights.astype(BF), 0, 0)
+            outs.append(out[head * HEAD_DIM : (head + 1) * HEAD_DIM] / total)
+            lse_ref[0, head : head + 1, i * BLOCK : n] = peak + jnp.log(total)
+        attended = jnp.concatenate(outs, axis=0).T.astype(BF)
+        half, slot = i // 2, (i % 2) ^ flip
+        rows = pl.ds(pl.multiple_of(slot * BLOCK, BLOCK), BLOCK)
+
+        @pl.when(half == core)
+        def _():
+            keep_ref[rows, :] = attended
+
+        @pl.when(half != core)
+        def _():
+            send_ref[rows, :] = attended
+
+
+def attend_back_kernel(
+    idx, q_ref, k_ref, v_ref, own_ref, other_ref, seg_row, seg_col, lse_ref, cosine, sine,
+    dq_ref, dk_ref, dv_ref, key_sum, value_sum,
+):
+    core, flip = idx[2], idx[3]
+    low_lanes = iota((BLOCK, 2 * HEAD_DIM), 1) < HEAD_DIM
+    key_sum[...] = jnp.zeros(key_sum.shape, F32)
+    value_sum[...] = jnp.zeros(value_sum.shape, F32)
+    for i in range(q_ref.shape[0] // BLOCK):
+        n = (i + 1) * BLOCK
+        queries = q_ref[i * BLOCK : n, :]
+        keys, values = k_ref[:n, :], v_ref[:n, :]
+        bias = mask_of(seg_row, seg_col, i)
+        half, slot = i // 2, (i % 2) ^ flip
+        rows = pl.ds(pl.multiple_of(slot * BLOCK, BLOCK), BLOCK)
+        grads = jnp.where(half == core, own_ref[rows, :], other_ref[rows, :])
+        grad_queries = []
+        for head in range(2):
+            mine = low_lanes if head == 0 else ~low_lanes
+            head_queries = jnp.where(mine, queries, 0)
+            head_grads = jnp.where(mine, grads, 0)
+            scores = dot(keys, head_queries, 1, 1) + bias
+            weights = jnp.exp(scores - lse_ref[0, head : head + 1, i * BLOCK : n])
+            grad_weights = dot(values, head_grads, 1, 1)
+            delta = jnp.sum(weights * grad_weights, axis=0, keepdims=True)
+            grad_scores = (weights * (grad_weights - delta)).astype(BF)
+            key_sum[:n, :] += dot(grad_scores, head_queries, 1, 0)
+            value_sum[:n, :] += dot(weights.astype(BF), head_grads, 1, 0)
+            grad_queries.append(dot(grad_scores, keys, 0, 0))
+        grad_query = jnp.where(low_lanes, grad_queries[0], grad_queries[1]) * HEAD_DIM**-0.5
+        tile = slice(i * BLOCK, n)
+        dq_ref[tile, :] = turn(grad_query, cosine[tile, :], sine[tile, :], -1.0).astype(BF)
+    for i in range(q_ref.shape[0] // BLOCK):
+        tile = slice(i * BLOCK, (i + 1) * BLOCK)
+        dk_ref[tile, :] = turn(key_sum[tile, :], cosine[tile, :], sine[tile, :], -1.0).astype(BF)
+        dv_ref[tile, :] = value_sum[tile, :].astype(BF)
+
+
+def routed_rows(small, routed):
+    index = iota((routed, small.shape[1]), 0).astype(F32)
+    return jnp.where((small[8:9, :] == index) | (small[9:10, :] == index), 1.0, 0.0)
+
+
+def ranks_of(named):
+    tokens = named.shape[1]
+    before, here = iota((tokens, tokens), 0), iota((tokens, tokens), 1)
+    earlier = (before < here) & (before // BLOCK == here // BLOCK)
+    stacked = jnp.concatenate([named, jnp.zeros_like(named)], axis=0).astype(BF)
+    return dot(stacked, jnp.where(earlier, 1.0, 0.0).astype(BF), 1, 0)[: named.shape[0]]
+
+
+def pick_row(values, index):
+    return jnp.sum(jnp.where(iota(values.shape, 0) == index, values, 0.0), axis=0, keepdims=True)
+
+
+def slots_of(named, rank, expert, capacity):
+    tokens = named.shape[1]
+    place = pick_row(rank, expert)
+    place = place + jnp.where(iota((1, tokens), 1) >= BLOCK, float(capacity), 0.0)
+    slot = iota((2 * capacity, tokens), 0).astype(F32)
+    taken = (slot == place) & (pick_row(named, expert) > 0.5)
+    return jnp.where(taken, 1.0, 0.0).astype(BF)
+
+
+def pair_of(first, second):
+    return jnp.concatenate([first[...], second[...]], axis=0)
+
+
+def grad_slots_kernel(idx, sa, sb, ca, cb, *outs):
+    small = jnp.concatenate([sa[...], sb[...]], axis=1)
+    named = routed_rows(small, 8)
+    rank = ranks_of(named)
+    grads = pair_of(ca, cb)
+    for k, out in enumerate(outs):
+        taken = slots_of(named, rank, idx[0] ^ k, out.shape[0] // 2)
+        out[...] = dot(taken, grads, 1, 0).astype(BF)
+
+
+def route_kernel(idx, keep, recv, xa, xb, params, sa, sb, *refs):
+    pieces, (hidden_ref, ow_ref, state_ref), outs = refs[:8], refs[8:11], refs[11:]
+    z, core = idx[1], idx[2]
+    depth = pieces[0].shape[0]
+    for (k, own), piece in zip(PIECES, pieces):
+        shard = lax.rem(z + k, RING) * 2 + (core if own else 1 - core)
+        ow_ref[pl.ds(pl.multiple_of(shard * depth, 16), depth), :] = piece[...]
+    width = keep.shape[1]
+    own_rows = pl.ds(pl.multiple_of(core * width, 16), width)
+    other_rows = pl.ds(pl.multiple_of((1 - core) * width, 16), width)
+    hidden = (
+        pair_of(xa, xb).astype(F32)
+        + dot(keep[...], ow_ref[own_rows, :], 1, 0)
+        + dot(recv[...], ow_ref[other_rows, :], 1, 0)
+    )
+    hidden_ref[...] = hidden
+    normed = (hidden * norm_scale(hidden) * params[15:16, :]).astype(BF)
+    small = jnp.concatenate([sa[...], sb[...]], axis=1)
+    logits = dot(params[...].astype(BF), normed, 1, 1)
+    named = routed_rows(small, 8)
+    rank = ranks_of(named)
+    shifted = logits[:8] + small[:8]
+    shifted = jnp.exp(shifted - jnp.max(shifted, axis=0, keepdims=True))
+    probabilities = shifted / jnp.sum(shifted, axis=0, keepdims=True)
+    mixed = []
+    for c in range(2):
+        first, second = logits[8 + 2 * c : 9 + 2 * c], logits[9 + 2 * c : 10 + 2 * c]
+        peak = jnp.maximum(first, second)
+        first, second = jnp.exp(first - peak), jnp.exp(second - peak)
+        mixed += [first / (first + second), second / (first + second)]
+    state_ref[0:8, :] = probabilities
+    state_ref[8:16, :] = rows_of(mixed, 8)
+    state_ref[16:24, :] = rank
+    slots = outs[0].shape[0] - 16
+    for k, out in enumerate(outs):
+        expert = idx[0] ^ k
+        taken = slots_of(named, rank, expert, slots // 2)
+        out[:slots, :] = dot(taken, normed, 1, 0).astype(BF)
+        gates = rows_of(split3(pick_row(probabilities, expert)), 16).astype(BF)
+        out[slots:, :] = jnp.zeros((16, out.shape[1]), BF)
+        out[slots:, :slots] = dot(gates, taken, 1, 1).astype(BF)
+
+
+def expert_kernel(idx, *refs):
+    tokens, grads, weights = refs[:8], refs[8:16], refs[16:24]
+    (t_ref, g_ref, inner_ref, gate_ref, up_ref, down_full) = refs[24:30]
+    outs = refs[30:38]
+    t_all, g_all, scale_all, gate_full, up_full, results = refs[38:]
+    core = idx[2]
+    j = pl.program_id(0)
+    slots = grads[0].shape[0]
+    half, chunk = weights[0].shape[1], weights[0].shape[2]
+
+    @pl.when(j == 0)
+    def _():
+        for k in range(RING):
+            columns = slice(k * chunk, (k + 1) * chunk)
+            for part in range(2):
+                rows = slice(part * half, (part + 1) * half)
+                piece = weights[2 * k + part]
+                gate_full[rows, columns] = piece[0]
+                up_full[rows, columns] = piece[1]
+                down_full[rows, columns] = piece[2]
+        for p in range(8):
+            rows = slice(p * slots, (p + 1) * slots)
+            t_all[rows, :] = tokens[p][:slots, :]
+            g_all[rows, :] = grads[p][...]
+            parts = tokens[p][slots:, :slots]
+            scale_all[rows, :] = dot(parts, jnp.ones((16, 128), BF), 0, 0)
+
+    tile = 2 * slots
+    rows = pl.ds(pl.multiple_of(j * tile, 16), tile)
+    entry, grad = t_all[rows, :], g_all[rows, :]
+    scale = scale_all[rows, :]
+    model = entry.shape[1]
+    t_ref[...] = entry
+    g_ref[...] = (grad.astype(F32) * wide(scale, model // 128)).astype(BF)
+    gate_act = dot(entry, gate_full[...], 1, 0)
+    up_act = dot(entry, up_full[...], 1, 0)
+    sigma = jax.nn.sigmoid(gate_act)
+    silu_act = gate_act * sigma
+    inner = (silu_act * up_act).astype(BF)
+    inner_ref[...] = inner
+    raw = dot(grad, down_full[...], 1, 0)
+    product = split2(inner.astype(F32) * raw)
+    grad_inner = raw * wide(scale, raw.shape[1] // 128)
+    grad_gate = (grad_inner * up_act * sigma * (1.0 + gate_act * (1.0 - sigma))).astype(BF)
+    grad_up = (grad_inner * silu_act).astype(BF)
+    gate_ref[...] = grad_gate
+    up_ref[...] = grad_up
+    entry_grad = dot(grad_gate, gate_full[...], 1, 1) + dot(grad_up, up_full[...], 1, 1)
+    ones = jnp.ones((16, raw.shape[1]), BF)
+    for part in range(2):
+        piece_rows = slice(part * slots, (part + 1) * slots)
+        result = results.at[2 * j + part]
+        result[:slots, :] = entry_grad[piece_rows].astype(BF)
+        sums = dot(ones, product[0][piece_rows], 1, 1) + dot(ones, product[1][piece_rows], 1, 1)
+        index = iota(sums.shape, 0)
+        high, middle, rest = split3(sums)
+        packed = jnp.where(
+            index == 4 * core,
+            high,
+            jnp.where(index == 4 * core + 1, middle, jnp.where(index == 4 * core + 2, rest, 0.0)),
+        )
+        result[slots:, :] = jnp.zeros((16, model), BF)
+        result[slots:, :slots] = packed.astype(BF)
+
+    @pl.when(j == pl.num_programs(0) - 1)
+    def _():
+        for p in range(8):
+            outs[p][...] = results[p]
+
+
+def expert_out_kernel(idx, inner_ref, down_ref, *outs):
+    j = pl.program_id(0)
+    slots = outs[0].shape[0]
+    out = dot(inner_ref[...], down_ref[...], 1, 1).astype(BF)
+    for step in range(4):
+
+        @pl.when(j == step)
+        def _(step=step):
+            outs[2 * step][...] = out[:slots]
+            outs[2 * step + 1][...] = out[slots:]
+
+
+def expert_grads_kernel(idx, t_ref, g_ref, inner_ref, gate_ref, up_ref, *outs):
+    k = pl.program_id(0)
+    half = outs[1].shape[1]
+    for step in range(RING):
+
+        @pl.when(k == step)
+        def _(step=step):
+            for place, (left, right) in enumerate(
+                ((t_ref, gate_ref), (t_ref, up_ref), (g_ref, inner_ref))
+            ):
+                grad = dot(left[...], right[...], 0, 0)
+                if step == 0:
+                    outs[0][place] = grad
+                else:
+                    outs[2 * step - 1][place] = grad[:half].astype(BF)
+                    outs[2 * step][place] = grad[half:].astype(BF)
+
+
+def slot_table(idx, small, state, capacity):
+    named = routed_rows(small, 8)
+    rank = state[16:24, :]
+    return [slots_of(named, rank, idx[0] ^ k, capacity) for k in range(RING)], named
+
+
+def branch_weights(state, named):
+    gates = state[0:8, :] * named
+    consts = [gates[6 + c : 7 + c] for c in range(2)]
+    normed_weight = gates[5:6]
+    for c in range(2):
+        normed_weight = normed_weight + consts[c] * state[8 + 2 * c : 9 + 2 * c, :]
+    vector_weights = [consts[c] * state[9 + 2 * c : 10 + 2 * c, :] for c in range(2)]
+    return consts, normed_weight, vector_weights
+
+
+def output_kernel(idx, hidden_ref, state_ref, sa, sb, params, *refs):
+    returned, (oa, ob) = refs[:4], refs[4:]
+    small = jnp.concatenate([sa[...], sb[...]], axis=1)
+    state = state_ref[...]
+    tables, named = slot_table(idx, small, state, returned[0].shape[0] // 2)
+    hidden = hidden_ref[...]
+    normed = hidden * norm_scale(hidden) * params[15:16, :]
+    _, normed_weight, vector_weights = branch_weights(state, named)
+    output = hidden + wide(column_of(normed_weight), normed.shape[1] // 128) * normed
+    vector_rows = rows_of(split3(params[12:13, :])[:2] * 2 + split3(params[13:14, :])[:2] * 2, 16)
+    first, second = split3(vector_weights[0])[:2], split3(vector_weights[1])[:2]
+    weight_rows = rows_of(
+        (first[0], first[0], first[1], first[1], second[0], second[0], second[1], second[1]), 16
+    )
+    output += dot(weight_rows.astype(BF), vector_rows.astype(BF), 0, 0)
+    for k in range(RING):
+        gate = pick_row(state[0:8, :], idx[0] ^ k)
+        high, low, _ = split3(gate)
+        table = tables[k].astype(F32)
+        output += dot((table * high).astype(BF), returned[k][...], 0, 0)
+        output += dot((table * low).astype(BF), returned[k][...], 0, 0)
+    oa[...] = output[:BLOCK].astype(BF)
+    ob[...] = output[BLOCK:].astype(BF)
+
+
+def hidden_back_kernel(idx, hidden_ref, state_ref, sa, sb, ca, cb, params, ow_ref, *refs):
+    returned = refs[:4]
+    gh_ref, low_ref, own_ref, send_ref, la, lb, small_ref = refs[4:]
+    core = idx[2]
+    small = jnp.concatenate([sa[...], sb[...]], axis=1)
+    state = state_ref[...]
+    slots = returned[0].shape[0] - 16
+    tables, named = slot_table(idx, small, state, slots // 2)
+    probabilities = state[0:8, :]
+    hidden = hidden_ref[...]
+    factor = norm_scale(hidden)
+    scaled_hidden = hidden * factor
+    normed = scaled_hidden * params[15:16, :]
+    normed_low = normed.astype(BF)
+    grads_low = pair_of(ca, cb)
+    grads = grads_low.astype(F32)
+    ones = jnp.ones((16, hidden.shape[1]), BF)
+    high, low = split2(grads * normed)
+    on_normed = (dot(ones, high, 1, 1) + dot(ones, low, 1, 1))[0:1]
+    first, second = split3(params[12:13, :])[:2], split3(params[13:14, :])[:2]
+    on_vectors = dot(rows_of(first + second, 16).astype(BF), grads_low, 1, 1)
+    on_vector = (on_vectors[0:1] + on_vectors[1:2], on_vectors[2:3] + on_vectors[3:4])
+    consts, normed_weight, vector_weights = branch_weights(state, named)
+    index = iota(probabilities.shape, 0)
+    grad_probs = jnp.where(index == 5, on_normed, 0.0)
+    mix_rows = []
+    for c in range(2):
+        mix_first, mix_second = state[8 + 2 * c : 9 + 2 * c, :], state[9 + 2 * c : 10 + 2 * c, :]
+        dot_c = mix_first * on_normed + mix_second * on_vector[c]
+        grad_probs = jnp.where(index == 6 + c, dot_c, grad_probs)
+        grad_first, grad_second = consts[c] * on_normed, consts[c] * on_vector[c]
+        mean = mix_first * grad_first + mix_second * grad_second
+        mix_rows += [mix_first * (grad_first - mean), mix_second * (grad_second - mean)]
+    back = jnp.zeros(hidden.shape, F32)
+    for k in range(RING):
+        packed = returned[k][slots:, :slots]
+        found = jnp.sum(dot(packed, tables[k], 1, 0), axis=0, keepdims=True)
+        grad_probs = jnp.where(index == (idx[0] ^ k), found, grad_probs)
+        back += dot(tables[k], returned[k][:slots, :], 0, 0)
+    grad_probs = grad_probs * named
+    grad_logits = probabilities * (
+        grad_probs - jnp.sum(probabilities * grad_probs, axis=0, keepdims=True)
+    )
+    la[...] = grad_logits[:, :BLOCK]
+    lb[...] = grad_logits[:, BLOCK:]
+    router_rows = jnp.concatenate([grad_logits, rows_of(mix_rows, 8)], axis=0)
+    rows_high, rows_low = split2(router_rows)
+    weights_low = params[...].astype(BF)
+    grad_normed = (
+        back
+        + dot(rows_high, weights_low, 0, 0)
+        + dot(rows_low, weights_low, 0, 0)
+        + wide(column_of(normed_weight), hidden.shape[1] // 128) * grads
+    )
+    router_grad = dot(rows_high, normed_low, 1, 0) + dot(rows_low, normed_low, 1, 0)
+    first, second = split3(vector_weights[0])[:2], split3(vector_weights[1])[:2]
+    vector_grad = dot(rows_of(first + second, 16).astype(BF), grads_low, 1, 0)
+    gain_grad = jnp.sum(grad_normed * scaled_hidden, axis=0, keepdims=True)
+    small_ref[...] = jnp.where(
+        iota(router_grad.shape, 0) < 12,
+        router_grad,
+        rows_of(
+            [jnp.zeros_like(gain_grad)] * 12
+            + [vector_grad[0:1] + vector_grad[1:2], vector_grad[2:3] + vector_grad[3:4], gain_grad],
+            16,
+        ),
+    )
+    scaled = grad_normed * params[15:16, :]
+    mean = jnp.mean(scaled * hidden, axis=-1, keepdims=True)
+    grad_hidden = grads + factor * scaled - hidden * (factor * factor * factor * mean)
+    gh_ref[...] = grad_hidden
+    grad_low = grad_hidden.astype(BF)
+    low_ref[...] = grad_low
+    width = own_ref.shape[1]
+    own_rows = pl.ds(pl.multiple_of(core * width, 16), width)
+    other_rows = pl.ds(pl.multiple_of((1 - core) * width, 16), width)
+    own_ref[...] = dot(grad_low, ow_ref[own_rows, :], 1, 1).astype(BF)
+    send_ref[...] = dot(grad_low, ow_ref[other_rows, :], 1, 1).astype(BF)
+
+
+def out_grad_kernel(idx, keep, recv, low_ref, small_ref, own_ref, send_ref, full):
+    z, core = idx[1], idx[2]
+    width, model = keep.shape[1], low_ref.shape[1]
+    own_rows = pl.ds(pl.multiple_of(core * width, 16), width)
+    other_rows = pl.ds(pl.multiple_of((1 - core) * width, 16), width)
+    full[own_rows, :model] = dot(keep[...], low_ref[...], 0, 0).astype(BF)
+    full[other_rows, :model] = dot(recv[...], low_ref[...], 0, 0).astype(BF)
+    eye = jnp.where(iota((16, 128), 0) == iota((16, 128), 1), 1.0, 0.0).astype(BF)
+    full[:, model:] = dot(small_ref[...].astype(BF), eye, 0, 0).astype(BF)
+    depth = own_ref.shape[1]
+    for k in range(RING):
+        shard = lax.rem(z + k, RING) * 2
+        own_ref[k] = full[pl.ds(pl.multiple_of((shard + core) * depth, 16), depth), :]
+        send_ref[k] = full[pl.ds(pl.multiple_of((shard + 1 - core) * depth, 16), depth), :]
+
+
+def project_back_kernel(idx, dq, dk, dv, normed_ref, x_ref, w_ref, *refs):
+    outs, (keep_ref, send_ref), full = refs[:7], refs[7:9], refs[9]
+    z, core, flip = idx[1], idx[2], idx[3]
+    width = dq.shape[1]
+    gain_sum = jnp.zeros((1, x_ref.shape[1]), F32)
+    for i in range(x_ref.shape[0] // BLOCK):
+        tile = slice(i * BLOCK, (i + 1) * BLOCK)
+        part = (
+            dot(dq[tile, :], w_ref[:, :width], 1, 1)
+            + dot(dk[tile, :], w_ref[:, width : 2 * width], 1, 1)
+            + dot(dv[tile, :], w_ref[:, 2 * width :], 1, 1)
+        )
+        x = x_ref[tile, :].astype(F32)
+        gain_sum += jnp.sum(part * (x * norm_scale(x)), axis=0, keepdims=True)
+        half, slot = i // 2, (i % 2) ^ flip
+        rows = pl.ds(pl.multiple_of(slot * BLOCK, BLOCK), BLOCK)
+
+        @pl.when(half == core)
+        def _(part=part, rows=rows):
+            keep_ref[rows, :] = part.astype(BF)
+
+        @pl.when(half != core)
+        def _(part=part, rows=rows):
+            send_ref[rows, :] = part.astype(BF)
+
+    for j, ref in enumerate((dq, dk, dv)):
+        full[:, j * width : (j + 1) * width] = dot(normed_ref[...], ref[...], 0, 0)
+    full[:, 3 * width :] = column_of(gain_sum)
+    depth = outs[1].shape[0]
+    for k in range(RING):
+        base = lax.rem(z + k, RING) * 2 * depth
+        first = full[pl.ds(pl.multiple_of(base, 16), depth), :]
+        second = full[pl.ds(pl.multiple_of(base + depth, 16), depth), :]
+        if k == 0:
+            outs[0][:depth, :] = first
+            outs[0][depth:, :] = second
+        else:
+            outs[2 * k - 1][...] = first.astype(BF)
+            outs[2 * k][...] = second.astype(BF)
+
+
+def input_back_kernel(idx, keep_ref, recv_ref, gh_ref, xa, xb, params, oa, ob):
+    gain = params[14:15, :]
+    for slot, (x_ref, out) in enumerate(((xa, oa), (xb, ob))):
+        tile = slice(slot * BLOCK, (slot + 1) * BLOCK)
+        x = x_ref[...].astype(F32)
+        factor = norm_scale(x)
+        scaled = (keep_ref[tile, :].astype(F32) + recv_ref[tile, :].astype(F32)) * gain
+        mean = jnp.mean(scaled * x, axis=-1, keepdims=True)
+        out[...] = (
+            gh_ref[tile, :] + factor * scaled - x * (factor * factor * factor * mean)
+        ).astype(BF)
+
+
+def up(values):
+    return lax.ppermute(values, "context", [(i, (i + 1) % RING) for i in range(RING)])
+
+
+def down(values):
+    return lax.ppermute(values, "context", [(i, (i - 1) % RING) for i in range(RING)])
+
+
+def across(values):
+    return lax.ppermute(values, "dp", [(0, 1), (1, 0)])
+
+
+def over(values, k):
+    return lax.ppermute(values, "experts", [(i, i ^ k) for i in range(RING)])
+
+
+def ring_gather(first, second):
+    from_below, from_above = (up(first), up(second)), (down(first), down(second))
+    opposite = (up(from_below[0]), down(from_above[1]))
+    return [(first, second), from_above, opposite, from_below]
+
+
+def ring_sum(own, pieces):
+    (above_1, above_2), (far_1, far_2), (below_1, below_2) = pieces
+    far_up, far_down = up(far_2), down(far_1)
+    got_1, got_2 = up(above_1), down(below_2)
+    more_2 = up((above_2.astype(F32) + far_up.astype(F32)).astype(BF))
+    more_1 = down((below_1.astype(F32) + far_down.astype(F32)).astype(BF))
+    return (
+        own[0] + got_1.astype(F32) + more_1.astype(F32),
+        own[1] + got_2.astype(F32) + more_2.astype(F32),
+    )
+
+
+def plane_sum(first, second):
+    a, b = first.astype(BF), second.astype(BF)
+    a, b = (a.astype(F32) + over(a, 1).astype(F32)), (b.astype(F32) + over(b, 2).astype(F32))
+    a_low, b_low = a.astype(BF), b.astype(BF)
+    return a + over(a_low, 2).astype(F32), b + over(b_low, 1).astype(F32)
+
+
+def chip_local(
+    inputs, cotangent, qkv_weight, out_weight, norm_gains, route_weight, const_gate, const_vec,
+    w_gate, w_up, w_down, prev_logits, routes, segments,
+):
+    e, z, core = lax.axis_index("experts"), lax.axis_index("context"), lax.axis_index("dp")
+    flip = z // 2
+    idx = jnp.stack([e, z, core, flip]).astype(jnp.int32)
+    odd = lax.rem(z, 2)
+    rows, model = inputs.shape[2], inputs.shape[3]
+    length = rows * RING
+    half_model = model // 2
+    capacity = rows * 5 // 16
+    slots = 2 * capacity
+
+    def place(z_index, d, which):
+        micro = z_index % 2 if which == 0 else 1 - z_index % 2
+        return (2 * micro + d) * 2 + z_index // 2
+
+    routes_of = [
+        [(zi * 2 + d, place(zi, d, which)) for zi in range(RING) for d in range(2)]
+        for which in range(2)
+    ]
+
+    def leave(values):
+        return [
+            lax.ppermute(
+                lax.dynamic_index_in_dim(values, odd if which == 0 else 1 - odd, 0, False),
+                ("context", "dp"),
+                routes_of[which],
+            )
+            for which in range(2)
+        ]
+
+    def come_home(first, second):
+        got = [
+            lax.ppermute(v, ("context", "dp"), [(b, a) for a, b in routes_of[which]])
+            for which, v in enumerate((first, second))
+        ]
+        return jnp.where(odd == 0, jnp.stack(got), jnp.stack(got[::-1]))
+
+    xa, xb = leave(inputs[:, 0])
+    small = jnp.concatenate(
+        [
+            jnp.swapaxes(prev_logits[:, 0], 1, 2),
+            jnp.swapaxes(routes[:, 0], 1, 2).astype(F32),
+            segments.astype(F32),
+            jnp.zeros((2, 5, rows), F32),
+        ],
+        axis=1,
+    )
+    sa, sb = leave(small)
+    ya, yb = across(xa), across(xb)
+    ta, tb = across(sa), across(sb)
+    seg = jnp.stack([sa[10], sb[10], ta[10], tb[10]]).reshape(2, 2, rows)
+    seg = jnp.where(core == 0, seg, seg[::-1])
+    seg = jnp.where(flip == 0, seg, seg[:, ::-1]).reshape(1, length)
+    seg_row, seg_col = jnp.broadcast_to(seg, (8, length)), seg.reshape(length, 1)
+
+    params = jnp.concatenate(
+        [route_weight.astype(F32).T, const_gate.astype(F32).T, const_vec, norm_gains], axis=0
+    )
+    other = across(params)
+    pair = jnp.where(core == 0, jnp.stack([params, other]), jnp.stack([other, params]))
+    ring = jnp.stack([pair, down(pair), up(up(pair)), up(pair)])
+    ring = lax.dynamic_slice_in_dim(jnp.concatenate([ring, ring]), RING - z, RING, 0)
+    params = jnp.transpose(ring, (2, 0, 1, 3)).reshape(16, model)
+
+    own_half = lax.dynamic_slice_in_dim(qkv_weight, core * half_model, half_model, 2)
+    other_half = lax.dynamic_slice_in_dim(qkv_weight, (1 - core) * half_model, half_model, 2)
+    qkv_pieces = [p for pieces in ring_gather(own_half, across(other_half)) for p in pieces]
+    below, above = up(out_weight), down(out_weight)
+    out_ring = [out_weight, above, up(below), below]
+    out_pieces = [p for piece in out_ring for p in (piece, across(piece))]
+
+    late = (cotangent[:, 0], w_gate[0], w_up[0], w_down[0])
+    late, _ = lax.optimization_barrier((late, (xa, xb)))
+    cot, gate_w, up_w, down_w = late
+    ca, cb = leave(cot)
+    mid = model // 2
+    first = jnp.stack([gate_w[:mid], up_w[:mid], down_w[:mid]])
+    second = jnp.stack([gate_w[mid:], up_w[mid:], down_w[mid:]])
+    expert_pieces = [p for pieces in ring_gather(first, second) for p in pieces]
+
+    cosine, sine = (jnp.asarray(t) for t in rope_tables(length))
+    q, k, v, normed_in, x_all, w_all = kernel_call(
+        project_kernel,
+        idx,
+        [xa, xb, ya, yb, params, cosine, sine, *qkv_pieces],
+        [((length, half_model), BF)] * 3
+        + [((length, model), BF)] * 2
+        + [((model, 3 * half_model), BF)],
+        flops=2 * length * model * 3 * half_model,
+    )
+    pairs = half_model // (2 * HEAD_DIM)
+    lanes = 2 * HEAD_DIM
+    by_pair = pl.BlockSpec((length, lanes), lambda h: (0, h))
+    half_by_pair = pl.BlockSpec((length // 2, lanes), lambda h: (0, h))
+    all_of = pl.BlockSpec(memory_space=pltpu.VMEM)
+    lse_spec = pl.BlockSpec((1, 8, length), lambda h: (h, 0, 0))
+    keep, send, lse = kernel_call(
+        attend_kernel,
+        idx,
+        [q, k, v, seg_row, seg_col],
+        [((length // 2, half_model), BF)] * 2 + [((pairs, 8, length), F32)],
+        flops=4 * length * length * half_model,
+        grid=(pairs,),
+        in_specs=[by_pair] * 3 + [all_of] * 2,
+        out_specs=[half_by_pair] * 2 + [lse_spec],
+    )
+    recv = across(send)
+
+    g_slots = kernel_call(
+        grad_slots_kernel,
+        idx,
+        [sa, sb, ca, cb],
+        [((slots, model), BF)] * RING,
+        flops=2 * RING * slots * 2 * rows * model,
+    )
+    g_mine = [g_slots[0]] + [over(g_slots[i], i) for i in range(1, RING)]
+    g_theirs = [across(g) for g in g_mine]
+    hidden, ow_all, state, *sent = kernel_call(
+        route_kernel,
+        idx,
+        [keep, recv, xa, xb, params, sa, sb, *out_pieces],
+        [((2 * rows, model), F32), ((model, model), BF), ((24, 2 * rows), F32)]
+        + [((slots + 16, model), BF)] * RING,
+        flops=2 * 2 * rows * model * model + 2 * RING * slots * 2 * rows * model,
+    )
+    t_mine = [sent[0]] + [over(sent[i], i) for i in range(1, RING)]
+    t_theirs = [across(t) for t in t_mine]
+
+    count = 8 * slots
+    hidden_units = RING * w_gate.shape[2]
+    tile_of = lambda n: pl.BlockSpec((2 * slots, n), lambda j: (j, 0))
+    t_all, g_all, inner, gate_g, up_g, down_all, *entry = kernel_call(
+        expert_kernel,
+        idx,
+        [*t_mine, *t_theirs, *g_mine, *g_theirs, *expert_pieces],
+        [((count, model), BF)] * 2
+        + [((count, hidden_units), BF)] * 3
+        + [((model, hidden_units), BF)]
+        + [((slots + 16, model), BF)] * 8,
+        flops=10 * count * model * hidden_units,
+        grid=(4,),
+        in_specs=[all_of] * 24,
+        out_specs=[tile_of(model)] * 2 + [tile_of(hidden_units)] * 3 + [all_of] * 9,
+        scratch=[
+            pltpu.VMEM((count, model), BF),
+            pltpu.VMEM((count, model), BF),
+            pltpu.VMEM((count, 128), F32),
+            pltpu.VMEM((model, hidden_units), BF),
+            pltpu.VMEM((model, hidden_units), BF),
+            pltpu.VMEM((8, slots + 16, model), BF),
+        ],
+    )
+
+    def give_back(parts):
+        sums = [
+            (parts[i].astype(F32) + across(parts[RING + i]).astype(F32)).astype(BF)
+            for i in range(RING)
+        ]
+        return [sums[0]] + [over(sums[i], i) for i in range(1, RING)]
+
+    entry_back = give_back(entry)
+    out_parts = kernel_call(
+        expert_out_kernel,
+        idx,
+        [inner, down_all],
+        [((slots, model), BF)] * 8,
+        flops=2 * count * model * hidden_units,
+        grid=(4,),
+        in_specs=[tile_of(hidden_units), all_of],
+        out_specs=[all_of] * 8,
+    )
+    out_back = give_back(out_parts)
+    chunk_of = pl.BlockSpec((count, w_gate.shape[2]), lambda j: (0, j))
+    own_grad, *far_grads = kernel_call(
+        expert_grads_kernel,
+        idx,
+        [t_all, g_all, inner, gate_g, up_g],
+        [((3, model, w_gate.shape[2]), F32)] + [((3, mid, w_gate.shape[2]), BF)] * 6,
+        flops=6 * count * model * hidden_units,
+        grid=(RING,),
+        in_specs=[all_of] * 2 + [chunk_of] * 3,
+        out_specs=[all_of] * 7,
+    )
+    grad_first, grad_second = ring_sum(
+        (own_grad[:, :mid], own_grad[:, mid:]),
+        [(far_grads[2 * i], far_grads[2 * i + 1]) for i in range(3)],
+    )
+    expert_grads = jnp.concatenate([grad_first, grad_second], axis=1)
+
+    grad_hidden, grad_low, ga_own, ga_send, la, lb, small_grad = kernel_call(
+        hidden_back_kernel,
+        idx,
+        [hidden, state, sa, sb, ca, cb, params, ow_all, *entry_back],
+        [((2 * rows, model), F32), ((2 * rows, model), BF)]
+        + [((2 * rows, half_model), BF)] * 2
+        + [((8, rows), F32)] * 2
+        + [((16, model), F32)],
+        flops=2 * 2 * rows * model * model + 2 * RING * slots * 2 * rows * model,
+    )
+    ga_other = across(ga_send)
+    logit_grad = jnp.swapaxes(come_home(la, lb), 1, 2)[:, None]
+    oa, ob = kernel_call(
+        output_kernel,
+        idx,
+        [hidden, state, sa, sb, params, *out_back],
+        [((rows, model), BF)] * 2,
+        flops=4 * RING * slots * 2 * rows * model,
+    )
+    output = come_home(oa, ob)[:, None]
+    og_own, og_send = kernel_call(
+        out_grad_kernel,
+        idx,
+        [keep, recv, grad_low, small_grad],
+        [((RING, model // 8, model + 128), BF)] * 2,
+        flops=2 * 2 * rows * model * model,
+        scratch=[pltpu.VMEM((model, model + 128), BF)],
+    )
+    og_sum = og_own.astype(F32) + across(og_send).astype(F32)
+    og_low = og_sum.astype(BF)
+    cut = model // 16
+    out_grad = ring_sum(
+        (og_sum[0, :cut], og_sum[0, cut:]),
+        [(og_low[i, :cut], og_low[i, cut:]) for i in range(1, RING)],
+    )
+    out_grad = jnp.concatenate(plane_sum(*out_grad), axis=0)
+    small_grad = out_grad[:, model : model + 16].T
+    grad_out = out_grad[:, :model]
+
+    dq, dk, dv = kernel_call(
+        attend_back_kernel,
+        idx,
+        [q, k, v, ga_own, ga_other, seg_row, seg_col, lse, cosine, sine],
+        [((length, half_model), BF)] * 3,
+        flops=10 * length * length * half_model,
+        grid=(pairs,),
+        in_specs=[by_pair] * 3 + [half_by_pair] * 2 + [all_of] * 2 + [lse_spec] + [all_of] * 2,
+        out_specs=[by_pair] * 3,
+        scratch=[pltpu.VMEM((length, lanes), F32)] * 2,
+    )
+    depth = model // 8
+    columns = 3 * half_model + 128
+    qkv_own, *rest = kernel_call(
+        project_back_kernel,
+        idx,
+        [dq, dk, dv, normed_in, x_all, w_all],
+        [((2 * depth, columns), F32)]
+        + [((depth, columns), BF)] * 6
+        + [((2 * rows, model), BF)] * 2,
+        flops=4 * length * model * 3 * half_model,
+        scratch=[pltpu.VMEM((model, columns), F32)],
+    )
+    far, gn_keep, gn_send = rest[:6], rest[6], rest[7]
+    ia, ib = kernel_call(
+        input_back_kernel,
+        idx,
+        [gn_keep, across(gn_send), grad_hidden, xa, xb, params],
+        [((rows, model), BF)] * 2,
+        flops=0,
+    )
+    input_grad = come_home(ia, ib).astype(F32)[:, None]
+    first, second = ring_sum(
+        (qkv_own[:depth], qkv_own[depth:]), [(far[2 * i], far[2 * i + 1]) for i in range(3)]
+    )
+    mine = jnp.where(core == 0, first, second)
+    theirs = across(jnp.where(core == 0, second, first).astype(BF)).astype(F32)
+    mine, theirs = plane_sum(mine, theirs)
+    left, right = jnp.where(core == 0, mine, theirs), jnp.where(core == 0, theirs, mine)
+    grad_qkv = jnp.stack(
+        [
+            jnp.concatenate(
+                [
+                    left[:, j * half_model : (j + 1) * half_model],
+                    right[:, j * half_model : (j + 1) * half_model],
+                ],
+                axis=1,
+            )
+            for j in range(3)
+        ]
+    )
+    gain_first = mine[:, 3 * half_model] + theirs[:, 3 * half_model]
+    grad_gain = jnp.stack([gain_first, small_grad[14]])
+    return (
+        output,
+        input_grad,
+        logit_grad,
+        grad_qkv,
+        grad_out,
+        grad_gain,
+        small_grad[:8].T,
+        small_grad[8:12].T,
+        small_grad[12:14],
+        expert_grads[0][None],
+        expert_grads[1][None],
+        expert_grads[2][None],
+    )
+
+
+def whole_sequence_fits(mesh):
+    return (mesh.shape["experts"], mesh.shape["context"], mesh.shape["dp"]) == (4, 4, 2)
+
+
 def solution(mesh):
+    local = chip_local if whole_sequence_fits(mesh) else general_local
     in_specs = (
         P(None, ("experts", "dp"), "context", None),
         P(None, ("experts", "dp"), "context", None),

time: 1110 us -> 465 us (0.42)
  waiting for transfers between devices: 463 us -> 153 us
  matrix products: 212 us -> 0 us
  local copies, waits for them, and re-layouts: 217 us -> 14.6 us
  Pallas kernels: 0 us -> 126 us
  starting transfers between devices: 33.8 us -> 148 us
  blocking collectives: 72.7 us -> 0 us
  other arithmetic: 86.7 us -> 16.4 us
  between operations: 17 us -> 2.05 us
    reduce_scatter x8 -> x0, waiting for transfers between devices: 232 us -> none  [the longest x2 61.3 us: local(): lax.psum_scatter(key_terms.reshape(total_keys, head_count, HEAD_DIM).asty...]
    dot_general x70 -> x0, matrix products: 212 us -> none  [the longest x2 27.5 us: local(): jnp.einsum('qjc,qcd->qjd', const_pick, const_out, precision=lax.Precision...]
    ppermute x0 -> x99, waiting for transfers between devices: none -> 153 us  [the longest x17 69 us: down(): lax.ppermute(values, 'context', [(i, (i - 1) % RING) for i in range(RING)])]
    ppermute x0 -> x99, starting transfers between devices: none -> 148 us  [the longest x19 50 us: up(): lax.ppermute(values, 'context', [(i, (i + 1) % RING) for i in range(RING)])]
    pallas_call x0 -> x13, Pallas kernels: none -> 126 us  [kernel_call(): pl.pallas_call(body, out_shape=[jax.ShapeDtypeStruct(s, d) for s, d in ou...]
    unnamed x28 -> x0, waiting for transfers between devices: 111 us -> none
    all_gather x9 -> x0, waiting for transfers between devices: 64.3 us -> none  [the longest x1 29.5 us: local(): lax.all_gather(qkv_weight, ('context', 'dp'), axis=1, tiled=True)]
    all_gather x6 -> x0, blocking collectives: 62.8 us -> none  [the longest x2 17.2 us: local(): segment_block = lax.all_gather(seg_rows, 'context', axis=0, tiled=True)]
  transfers between devices with their start and end apart: 31 -> 99, of which waited for: 17 -> 30; matrix products, arithmetic and copies ran while one was open for 36% -> 4% of each run, Pallas kernels for 0% -> 22%
where the time goes in v1:
time: 465 us; the launch traced here: 460 us
  waiting for transfers between devices  153 us (33%)
  starting transfers between devices  148 us (32%)
  Pallas kernels  126 us (27%)
  other arithmetic  16.4 us (4%)
  local copies, waits for them, and re-layouts  14.6 us (3%)
    pallas_call x13, Pallas kernels, kernel_call(): pl.pallas_call(body, out_shape=[jax.ShapeDtypeStruct(s, d) for s, d in ou...  126 us
    ppermute x17, waiting for transfers between devices, down(): lax.ppermute(values, 'context', [(i, (i - 1) % RING) for i in range(RING)])  69 us
    ppermute x19, starting transfers between devices, up(): lax.ppermute(values, 'context', [(i, (i + 1) % RING) for i in range(RING)])  50 us
    ppermute x20, waiting for transfers between devices, over(): return lax.ppermute(values, 'experts', [(i, i ^ k) for i in range(RING)])  29.6 us
    ppermute x17, starting transfers between devices, down(): lax.ppermute(values, 'context', [(i, (i - 1) % RING) for i in range(RING)])  29.3 us
    ppermute x6, waiting for transfers between devices, come_home(): lax.ppermute(v, ('context', 'dp'), [(b, a) for a, b in routes_of[which]])  27.7 us
    ppermute x31, starting transfers between devices, across(): return lax.ppermute(values, 'dp', [(0, 1), (1, 0)])  27.2 us
    ppermute x20, starting transfers between devices, over(): return lax.ppermute(values, 'experts', [(i, i ^ k) for i in range(RING)])  24.7 us
  transfers between devices with their start and end apart: 99, of which 30 were waited for; matrix products, arithmetic and copies ran while one was open for 4% of the time, Pallas kernels for 22%

profile of v1, /device:TPU:0, one launch (start us, length us, event | category | flops | bytes accessed | tf_op | source)
XLA Modules:
  0.0 460.1 jit_solution(14784672888856004505)
XLA Ops:
  22.9 8.4 %collective-permute-done.7 = f32[2,16,96]{2,1,0:T(8,128)S(1)} collective-permute-done((f32[2,16,96]{2,1,0:T(8,128)S(1)}, f32[2,16,96]{2,1,0:T(8,128)S(1)}, u32[]{:S(2)}, u32[]{:S(2)}) %collective-permute-start.7) | collective-permute-done | bytes 12320 | tf_op jit(solution)/shard_map/ppermute | solution.py:1032
  38.7 8.9 %collective-permute-start.11 = (bf16[3,96,384]{2,1,0:T(8,128)(2,1)}, bf16[3,96,384]{2,1,0:T(8,128)(2,1)S(1)}, u32[]{:S(2)}, u32[]{:S(2)}) collective-permute-start(bf16[3,96,384]{2,1,0:T(8,128)(2,1)} %get-tuple-element.235.refs_0_), channel_id=1, source_target_pairs={{0,2},{2,4},{4,6},{6,0},{1,3},{3,5},{5,7},{7,1},{8,10},{10,12},{12... | collective-permute-start | bytes 663560 | tf_op jit(solution)/shard_map/ppermute | solution.py:1032
  67.1 8.3 %collective-permute-done.10.refs_3_ = bf16[3,96,384]{2,1,0:T(8,128)(2,1)S(1)} collective-permute-done((bf16[3,96,384]{2,1,0:T(8,128)(2,1)S(1)}, bf16[3,96,384]{2,1,0:T(8,128)(2,1)S(1)}, u32[]{:S(2)}, u32[]{:S(2)}) %collective-permute-start.10) | collective-permute-done | bytes 221216 | tf_op jit(solution)/shard_map/ppermute | solution.py:1036
  79.1 5.8 %collective-permute-done.13.refs_5_ = bf16[3,96,384]{2,1,0:T(8,128)(2,1)S(1)} collective-permute-done((bf16[3,96,384]{2,1,0:T(8,128)(2,1)S(1)}, bf16[3,96,384]{2,1,0:T(8,128)(2,1)S(1)}, u32[]{:S(2)}, u32[]{:S(2)}) %collective-permute-start.13) | collective-permute-done | bytes 221216 | tf_op jit(solution)/shard_map/ppermute | solution.py:1036
  84.9 7.8 %collective-permute-start.45 = (bf16[3,384,256]{2,1,0:T(8,128)(2,1)S(1)}, bf16[3,384,256]{2,1,0:T(8,128)(2,1)}, u32[]{:S(2)}, u32[]{:S(2)}) collective-permute-start(bf16[3,384,256]{2,1,0:T(8,128)(2,1)S(1)} %pad_maximum_fusion.2.refs_16_), channel_id=1, source_target_pairs={{0,2},{2,4},{4,6},{6,0},{1,3},{3,5},{5,7},{7,1},{8,10},{10,12},{12... | collective-permute-start | bytes 1769480 | tf_op jit(solution)/shard_map/ppermute | solution.py:1032
  95.6 8.4 %shard_map.247 = (bf16[1024,384]{1,0:T(8,128)(2,1)}, bf16[1024,384]{1,0:T(8,128)(2,1)}, bf16[1024,384]{1,0:T(8,128)(2,1)}, bf16[1024,768]{1,0:T(8,128)(2,1)}, bf...) custom-call(s32[4]{0:T(128)} %pad_add_fusion.idx, bf16[256,768]{1,0:T(8,128)(2,1)} %copy-done.12, ...), custom_call_target="tpu_custom_call" | custom-call | flops 1811939328 | bytes 11714560 | tf_op jit(solution)/shard_map/pallas_call | solution.py:513
  109.4 16.2 %shard_map.248 = (bf16[512,384]{1,0:T(8,128)(2,1)}, bf16[512,384]{1,0:T(8,128)(2,1)}, f32[3,8,1024]{2,1,0:T(8,128)}) custom-call(s32[4]{0:T(128)} %pad_add_fusion.idx, bf16[1024,384]{1,0:T(8,128)(2,1)} %get-tuple-element.90.q_ref, bf16[1024,384]{1,0:T(8,128)(2,1)} %get-tuple-element.91.k_ref, bf16[1024,384]{1,0:T(8,128)(2,1)} %get-tuple-element.92.v_ref, ...), custom_call_target="tpu_custom_call" | custom-call | flops 1610612736 | bytes 3280896 | tf_op jit(solution)/shard_map/pallas_call | solution.py:513
  130.6 6.6 %collective-permute-done.43.refs_18_ = bf16[3,384,256]{2,1,0:T(8,128)(2,1)S(1)} collective-permute-done((bf16[3,384,256]{2,1,0:T(8,128)(2,1)S(1)}, bf16[3,384,256]{2,1,0:T(8,128)(2,1)S(1)}, u32[]{:S(2)}, u32[]{:S(2)}) %collective-permute-start.43) | collective-permute-done | bytes 589856 | tf_op jit(solution)/shard_map/ppermute | solution.py:1036
  149.0 10.1 %collective-permute-start.46 = (bf16[3,384,256]{2,1,0:T(8,128)(2,1)}, bf16[3,384,256]{2,1,0:T(8,128)(2,1)S(1)}, u32[]{:S(2)}, u32[]{:S(2)}) collective-permute-start(bf16[3,384,256]{2,1,0:T(8,128)(2,1)} %collective-permute-done.45.refs_22_), channel_id=1, source_target_pairs={{0,2},{2,4},{4,6},{6,0},{1,3},{3,5},{5,7},{7,1},{8,10},{10,12},{12... | collective-permute-start | bytes 1769480 | tf_op jit(solution)/shard_map/ppermute | solution.py:1032
  162.2 11.3 %collective-permute-done.28.refs_2_ = bf16[176,768]{1,0:T(8,128)(2,1)S(1)} collective-permute-done((bf16[176,768]{1,0:T(8,128)(2,1)}, bf16[176,768]{1,0:T(8,128)(2,1)S(1)}, u32[]{:S(2)}, u32[]{:S(2)}) %collective-permute-start.28) | collective-permute-done | bytes 270368 | tf_op jit(solution)/shard_map/ppermute | solution.py:1044
  174.1 10.8 %collective-permute-done.47.refs_21_ = bf16[3,384,256]{2,1,0:T(8,128)(2,1)S(1)} collective-permute-done((bf16[3,384,256]{2,1,0:T(8,128)(2,1)S(1)}, bf16[3,384,256]{2,1,0:T(8,128)(2,1)S(1)}, u32[]{:S(2)}, u32[]{:S(2)}) %collective-permute-start.47) | collective-permute-done | bytes 589856 | tf_op jit(solution)/shard_map/ppermute | solution.py:1036
  185.8 22.6 %shard_map.251 = (bf16[1280,768]{1,0:T(8,128)(2,1)}, bf16[1280,768]{1,0:T(8,128)(2,1)}, bf16[1280,1024]{1,0:T(8,128)(2,1)}, bf16[1280,1024]{1,0:T(8,128)(2,1)}, ...) custom-call(s32[4]{0:T(128)} %pad_add_fusion.idx, ...), custom_call_target="tpu_custom_call" | custom-call | flops 10066329600 | bytes 24379392 | tf_op jit(solution)/shard_map/pallas_call | solution.py:513
  209.1 6.4 %shard_map.252 = (bf16[160,768]{1,0:T(8,128)(2,1)}, bf16[160,768]{1,0:T(8,128)(2,1)}, bf16[160,768]{1,0:T(8,128)(2,1)}, bf16[160,768]{1,0:T(8,128)(2,1)}, bf16[1...) custom-call(s32[4]{0:T(128)} %pad_add_fusion.idx, ...), custom_call_target="tpu_custom_call" | custom-call | flops 2013265920 | bytes 6160384 | tf_op jit(solution)/shard_map/pallas_call | solution.py:513
  216.0 13.0 %shard_map.259 = (f32[3,768,256]{2,1,0:T(8,128)}, bf16[3,384,256]{2,1,0:T(8,128)(2,1)}, bf16[3,384,256]{2,1,0:T(8,128)(2,1)}, bf16[3,384,256]{2,1,0:T(8,128)(2,1...) custom-call(s32[4]{0:T(128)} %pad_add_fusion.idx, ...), custom_call_target="tpu_custom_call" | custom-call | flops 6039797760 | bytes 17694720 | tf_op jit(solution)/shard_map/pallas_call | solution.py:513
  263.1 7.3 %shard_map.254 = (f32[512,768]{1,0:T(8,128)}, bf16[512,768]{1,0:T(8,128)(2,1)}, bf16[512,384]{1,0:T(8,128)(2,1)}, bf16[512,384]{1,0:T(8,128)(2,1)}, f32[8,256]{1...) custom-call(s32[4]{0:T(128)} %pad_add_fusion.idx, f32[512,768]{1,0:T(8,128)} %get-tuple-element.95.hidden_ref, ...), custom_call_target="tpu_custom_call" | custom-call | flops 1107296256 | bytes 7962624 | tf_op jit(solution)/shard_map/pallas_call | solution.py:513
  286.1 13.7 %collective-permute-start.82 = (bf16[4,96,896]{2,1,0:T(8,128)(2,1)}, bf16[4,96,896]{2,1,0:T(8,128)(2,1)S(1)}, u32[]{:S(2)}, u32[]{:S(2)}) collective-permute-start(bf16[4,96,896]{2,1,0:T(8,128)(2,1)} %get-tuple-element.156), channel_id=1, source_target_pairs={{0,1},{1,0},{2,3},{3,2},{4,5},{5,4},{6,7},{7,6},{8,9},{9,8},{10,11... | collective-permute-start | bytes 2064392 | tf_op jit(solution)/shard_map/ppermute | solution.py:1040
  299.8 9.8 %collective-permute-done.57 = bf16[256,768]{1,0:T(8,128)(2,1)S(1)} collective-permute-done((bf16[256,768]{1,0:T(8,128)(2,1)S(1)}, bf16[256,768]{1,0:T(8,128)(2,1)S(1)}, u32[]{:S(2)}, u32[]{:S(2)}) %collective-permute-start.57) | collective-permute-done | bytes 393248 | tf_op jit(solution)/shard_map/ppermute | solution.py:1107
  311.3 19.0 %shard_map.255 = (bf16[1024,384]{1,0:T(8,128)(2,1)}, bf16[1024,384]{1,0:T(8,128)(2,1)}, bf16[1024,384]{1,0:T(8,128)(2,1)}) custom-call(s32[4]{0:T(128)} %pad_add_fusion.idx, bf16[1024,384]{1,0:T(8,128)(2,1)} %get-tuple-element.90.q_ref, bf16[1024,384]{1,0:T(8,128)(2,1)} %get-tuple-element.91.k_ref, bf16[1024,384]{1,0:T(8,128)(2,1)} %get-tuple-element.92.v_ref, ...), custom_call_target="tpu_custom_call" | custom-call | flops 4026531840 | bytes 6688768 | tf_op jit(solution)/shard_map/pallas_call | solution.py:513
  330.4 13.5 %shard_map.256 = (f32[192,1280]{1,0:T(8,128)}, bf16[96,1280]{1,0:T(8,128)(2,1)}, bf16[96,1280]{1,0:T(8,128)(2,1)}, bf16[96,1280]{1,0:T(8,128)(2,1)}, bf16[96,128...) custom-call(s32[4]{0:T(128)} %pad_add_fusion.idx, ...), custom_call_target="tpu_custom_call" | custom-call | flops 3623878656 | bytes 11304960 | tf_op jit(solution)/shard_map/pallas_call | solution.py:513
  350.2 9.3 %collective-permute-start.89 = (bf16[48,896]{1,0:T(8,128)(2,1)S(1)}, bf16[48,896]{1,0:T(8,128)(2,1)S(1)}, u32[]{:S(2)}, u32[]{:S(2)}) collective-permute-start(bf16[48,896]{1,0:T(8,128)(2,1)S(1)} %get-tuple-element.223), channel_id=1, source_target_pairs={{0,2},{2,4},{4,6},{6,0},{1,3},{3,5},{5,7},{7,1},{8,10},{10,12},{12... | collective-permute-start | bytes 258056 | tf_op jit(solution)/shard_map/ppermute | solution.py:1032
  363.9 15.0 %collective-permute-done.84 = bf16[48,896]{1,0:T(8,128)(2,1)S(1)} collective-permute-done((bf16[48,896]{1,0:T(8,128)(2,1)S(1)}, bf16[48,896]{1,0:T(8,128)(2,1)S(1)}, u32[]{:S(2)}, u32[]{:S(2)}) %collective-permute-start.84) | collective-permute-done | bytes 86048 | tf_op jit(solution)/shard_map/ppermute | solution.py:1036
  385.3 8.9 %collective-permute-done.88 = bf16[48,896]{1,0:T(8,128)(2,1)S(1)} collective-permute-done((bf16[48,896]{1,0:T(8,128)(2,1)S(1)}, bf16[48,896]{1,0:T(8,128)(2,1)S(1)}, u32[]{:S(2)}, u32[]{:S(2)}) %collective-permute-start.88) | collective-permute-done | bytes 86048 | tf_op jit(solution)/shard_map/ppermute | solution.py:1036
  403.9 7.5 %collective-permute-done.85 = bf16[48,896]{1,0:T(8,128)(2,1)S(1)} collective-permute-done((bf16[48,896]{1,0:T(8,128)(2,1)S(1)}, bf16[48,896]{1,0:T(8,128)(2,1)S(1)}, u32[]{:S(2)}, u32[]{:S(2)}) %collective-permute-start.85) | collective-permute-done | bytes 86048 | tf_op jit(solution)/shard_map/ppermute | solution.py:1036
  438.5 18.0 %collective-permute-done.68 = bf16[256,768]{1,0:T(8,128)(2,1)S(1)} collective-permute-done((bf16[256,768]{1,0:T(8,128)(2,1)}, bf16[256,768]{1,0:T(8,128)(2,1)S(1)}, u32[]{:S(2)}, u32[]{:S(2)}) %collective-permute-start.68) | collective-permute-done | bytes 393248 | tf_op jit(solution)/shard_map/ppermute | solution.py:1107
  (422 shorter events, 191.7 us)
Async XLA Ops:
  11.1 36.5 %collective-permute-start.21 = (bf16[96,768]{1,0:T(8,128)(2,1)}, bf16[96,768]{1,0:T(8,128)(2,1)}, u32[]{:S(2)}, u32[]{:S(2)}) collective-permute-start(bf16[96,768]{1,0:T(8,128)(2,1)} %refs_0_.1), channel_id=1, source_target_pairs={{0,6},{2,0},{4,2},{6,4},{1,7},{3,1},{5,3},{7,5},{8,14},{10,8},{12,... | collective-permute-start | bytes 442376 | tf_op jit(solution)/shard_map/ppermute | solution.py:1036
  20.2 31.8 %collective-permute-start.20 = (bf16[96,768]{1,0:T(8,128)(2,1)}, bf16[96,768]{1,0:T(8,128)(2,1)}, u32[]{:S(2)}, u32[]{:S(2)}) collective-permute-start(bf16[96,768]{1,0:T(8,128)(2,1)} %refs_0_.1), channel_id=1, source_target_pairs={{0,1},{1,0},{2,3},{3,2},{4,5},{5,4},{6,7},{7,6},{8,9},{9,8},{10,11... | collective-permute-start | bytes 442376 | tf_op jit(solution)/shard_map/ppermute | solution.py:1040
  66.1 26.6 %collective-permute-start.3 = (bf16[256,768]{1,0:T(8,128)(2,1)S(1)}, bf16[256,768]{1,0:T(8,128)(2,1)S(1)}, u32[]{:S(2)}, u32[]{:S(2)}) collective-permute-start(bf16[256,768]{1,0:T(8,128)(2,1)S(1)} %collective-permute-done.1.xb), channel_id=1, source_target_pairs={{0,1},{1,0},{2,3},{3,2},{4,5},{5,4},{6,7},{7,6},{8,9},{9,8},{10,11... | collective-permute-start | bytes 1179656 | tf_op jit(solution)/shard_map/ppermute | solution.py:1040
  66.2 26.6 %collective-permute-start.2 = (bf16[256,768]{1,0:T(8,128)(2,1)S(1)}, bf16[256,768]{1,0:T(8,128)(2,1)S(1)}, u32[]{:S(2)}, u32[]{:S(2)}) collective-permute-start(bf16[256,768]{1,0:T(8,128)(2,1)S(1)} %collective-permute-done.xa), channel_id=1, source_target_pairs={{0,1},{1,0},{2,3},{3,2},{4,5},{5,4},{6,7},{7,6},{8,9},{9,8},{10,11... | collective-permute-start | bytes 1179656 | tf_op jit(solution)/shard_map/ppermute | solution.py:1040
  76.6 31.9 %collective-permute-start.35 = (bf16[256,768]{1,0:T(8,128)(2,1)S(1)}, bf16[256,768]{1,0:T(8,128)(2,1)S(1)}, u32[]{:S(2)}, u32[]{:S(2)}) collective-permute-start(bf16[256,768]{1,0:T(8,128)(2,1)S(1)} %get-tuple-element.218), channel_id=1, source_target_pairs={{0,4},{1,6},{2,0},{3,2},{4,5},{5,7},{6,1},{7,3},{8,12},{9,14},{10,... | collective-permute-start | bytes 1179656 | tf_op jit(solution)/shard_map/ppermute | solution.py:1097
  78.4 47.2 %collective-permute-start.34 = (bf16[256,768]{1,0:T(8,128)(2,1)S(1)}, bf16[256,768]{1,0:T(8,128)(2,1)S(1)}, u32[]{:S(2)}, u32[]{:S(2)}) collective-permute-start(bf16[256,768]{1,0:T(8,128)(2,1)S(1)} %get-tuple-element.219), channel_id=1, source_target_pairs={{0,0},{1,2},{2,4},{3,6},{4,1},{5,3},{6,5},{7,7},{8,8},{9,10},{10,1... | collective-permute-start | bytes 1179656 | tf_op jit(solution)/shard_map/ppermute | solution.py:1097
  84.9 44.2 %collective-permute-start.45 = (bf16[3,384,256]{2,1,0:T(8,128)(2,1)S(1)}, bf16[3,384,256]{2,1,0:T(8,128)(2,1)}, u32[]{:S(2)}, u32[]{:S(2)}) collective-permute-start(bf16[3,384,256]{2,1,0:T(8,128)(2,1)S(1)} %pad_maximum_fusion.2.refs_16_), channel_id=1, source_target_pairs={{0,2},{2,4},{4,6},{6,0},{1,3},{3,5},{5,7},{7,1},{8,10},{10,12},{12... | collective-permute-start | bytes 1769480 | tf_op jit(solution)/shard_map/ppermute | solution.py:1032
  92.8 44.4 %collective-permute-start.43 = (bf16[3,384,256]{2,1,0:T(8,128)(2,1)S(1)}, bf16[3,384,256]{2,1,0:T(8,128)(2,1)S(1)}, u32[]{:S(2)}, u32[]{:S(2)}) collective-permute-start(bf16[3,384,256]{2,1,0:T(8,128)(2,1)S(1)} %pad_maximum_fusion.2.refs_16_), channel_id=1, source_target_pairs={{0,6},{2,0},{4,2},{6,4},{1,7},{3,1},{5,3},{7,5},{8,14},{10,8},{12,... | collective-permute-start | bytes 1769480 | tf_op jit(solution)/shard_map/ppermute | solution.py:1036
  94.3 44.4 %collective-permute-start.48 = (bf16[3,384,256]{2,1,0:T(8,128)(2,1)S(1)}, bf16[3,384,256]{2,1,0:T(8,128)(2,1)}, u32[]{:S(2)}, u32[]{:S(2)}) collective-permute-start(bf16[3,384,256]{2,1,0:T(8,128)(2,1)S(1)} %pad_maximum_fusion.3.refs_17_), channel_id=1, source_target_pairs={{0,2},{2,4},{4,6},{6,0},{1,3},{3,5},{5,7},{7,1},{8,10},{10,12},{12... | collective-permute-start | bytes 1769480 | tf_op jit(solution)/shard_map/ppermute | solution.py:1032
  108.5 38.4 %collective-permute-start.44 = (bf16[3,384,256]{2,1,0:T(8,128)(2,1)S(1)}, bf16[3,384,256]{2,1,0:T(8,128)(2,1)S(1)}, u32[]{:S(2)}, u32[]{:S(2)}) collective-permute-start(bf16[3,384,256]{2,1,0:T(8,128)(2,1)S(1)} %pad_maximum_fusion.3.refs_17_), channel_id=1, source_target_pairs={{0,6},{2,0},{4,2},{6,4},{1,7},{3,1},{5,3},{7,5},{8,14},{10,8},{12,... | collective-permute-start | bytes 1769480 | tf_op jit(solution)/shard_map/ppermute | solution.py:1036
  208.4 31.8 %collective-permute-start.58 = (bf16[176,768]{1,0:T(8,128)(2,1)}, bf16[176,768]{1,0:T(8,128)(2,1)S(1)}, u32[]{:S(2)}, u32[]{:S(2)}) collective-permute-start(bf16[176,768]{1,0:T(8,128)(2,1)} %get-tuple-element.123), channel_id=1, source_target_pairs={{0,1},{1,0},{2,3},{3,2},{4,5},{5,4},{6,7},{7,6},{8,9},{9,8},{10,11... | collective-permute-start | bytes 811016 | tf_op jit(solution)/shard_map/ppermute | solution.py:1040
  208.5 27.8 %collective-permute-start.59 = (bf16[176,768]{1,0:T(8,128)(2,1)}, bf16[176,768]{1,0:T(8,128)(2,1)S(1)}, u32[]{:S(2)}, u32[]{:S(2)}) collective-permute-start(bf16[176,768]{1,0:T(8,128)(2,1)} %get-tuple-element.125), channel_id=1, source_target_pairs={{0,1},{1,0},{2,3},{3,2},{4,5},{5,4},{6,7},{7,6},{8,9},{9,8},{10,11... | collective-permute-start | bytes 811016 | tf_op jit(solution)/shard_map/ppermute | solution.py:1040
  209.0 28.9 %collective-permute-start.61 = (bf16[176,768]{1,0:T(8,128)(2,1)}, bf16[176,768]{1,0:T(8,128)(2,1)S(1)}, u32[]{:S(2)}, u32[]{:S(2)}) collective-permute-start(bf16[176,768]{1,0:T(8,128)(2,1)} %get-tuple-element.127), channel_id=1, source_target_pairs={{0,1},{1,0},{2,3},{3,2},{4,5},{5,4},{6,7},{7,6},{8,9},{9,8},{10,11... | collective-permute-start | bytes 811016 | tf_op jit(solution)/shard_map/ppermute | solution.py:1040
  231.8 50.6 %collective-permute-start.94 = (bf16[3,384,256]{2,1,0:T(8,128)(2,1)}, bf16[3,384,256]{2,1,0:T(8,128)(2,1)S(1)}, u32[]{:S(2)}, u32[]{:S(2)}) collective-permute-start(bf16[3,384,256]{2,1,0:T(8,128)(2,1)} %get-tuple-element.164), channel_id=1, source_target_pairs={{0,6},{2,0},{4,2},{6,4},{1,7},{3,1},{5,3},{7,5},{8,14},{10,8},{12,... | collective-permute-start | bytes 1769480 | tf_op jit(solution)/shard_map/ppermute | solution.py:1036
  252.9 31.3 %collective-permute-start.97 = (bf16[3,384,256]{2,1,0:T(8,128)(2,1)}, bf16[3,384,256]{2,1,0:T(8,128)(2,1)S(1)}, u32[]{:S(2)}, u32[]{:S(2)}) collective-permute-start(bf16[3,384,256]{2,1,0:T(8,128)(2,1)} %get-tuple-element.167), channel_id=1, source_target_pairs={{0,2},{2,4},{4,6},{6,0},{1,3},{3,5},{5,7},{7,1},{8,10},{10,12},{12... | collective-permute-start | bytes 1769480 | tf_op jit(solution)/shard_map/ppermute | solution.py:1032
  257.7 121.7 %collective-permute-start.93 = (bf16[3,384,256]{2,1,0:T(8,128)(2,1)}, bf16[3,384,256]{2,1,0:T(8,128)(2,1)S(1)}, u32[]{:S(2)}, u32[]{:S(2)}) collective-permute-start(bf16[3,384,256]{2,1,0:T(8,128)(2,1)} %get-tuple-element.162), channel_id=1, source_target_pairs={{0,2},{2,4},{4,6},{6,0},{1,3},{3,5},{5,7},{7,1},{8,10},{10,12},{12... | collective-permute-start | bytes 1769480 | tf_op jit(solution)/shard_map/ppermute | solution.py:1032
  276.0 106.9 %collective-permute-start.96 = (bf16[3,384,256]{2,1,0:T(8,128)(2,1)}, bf16[3,384,256]{2,1,0:T(8,128)(2,1)S(1)}, u32[]{:S(2)}, u32[]{:S(2)}) collective-permute-start(bf16[3,384,256]{2,1,0:T(8,128)(2,1)} %get-tuple-element.165), channel_id=1, source_target_pairs={{0,6},{2,0},{4,2},{6,4},{1,7},{3,1},{5,3},{7,5},{8,14},{10,8},{12,... | collective-permute-start | bytes 1769480 | tf_op jit(solution)/shard_map/ppermute | solution.py:1036
  282.4 27.1 %collective-permute-start.57 = (bf16[256,768]{1,0:T(8,128)(2,1)S(1)}, bf16[256,768]{1,0:T(8,128)(2,1)S(1)}, u32[]{:S(2)}, u32[]{:S(2)}) collective-permute-start(bf16[256,768]{1,0:T(8,128)(2,1)S(1)} %copy-done.39), channel_id=1, source_target_pairs={{4,0},{6,1},{0,2},{2,3},{5,4},{7,5},{1,6},{3,7},{12,8},{14,9},{8,1... | collective-permute-start | bytes 1179656 | tf_op jit(solution)/shard_map/ppermute | solution.py:1107
  284.3 26.4 %collective-permute-start.65 = (bf16[512,384]{1,0:T(8,128)(2,1)S(1)}, bf16[512,384]{1,0:T(8,128)(2,1)S(1)}, u32[]{:S(2)}, u32[]{:S(2)}) collective-permute-start(bf16[512,384]{1,0:T(8,128)(2,1)S(1)} %copy-done.40), channel_id=1, source_target_pairs={{0,1},{1,0},{2,3},{3,2},{4,5},{5,4},{6,7},{7,6},{8,9},{9,8},{10,11... | collective-permute-start | bytes 1179656 | tf_op jit(solution)/shard_map/ppermute | solution.py:1040
  286.1 58.7 %collective-permute-start.82 = (bf16[4,96,896]{2,1,0:T(8,128)(2,1)}, bf16[4,96,896]{2,1,0:T(8,128)(2,1)S(1)}, u32[]{:S(2)}, u32[]{:S(2)}) collective-permute-start(bf16[4,96,896]{2,1,0:T(8,128)(2,1)} %get-tuple-element.156), channel_id=1, source_target_pairs={{0,1},{1,0},{2,3},{3,2},{4,5},{5,4},{6,7},{7,6},{8,9},{9,8},{10,11... | collective-permute-start | bytes 2064392 | tf_op jit(solution)/shard_map/ppermute | solution.py:1040
  309.5 73.4 %collective-permute-start.95 = (bf16[3,384,256]{2,1,0:T(8,128)(2,1)S(1)}, bf16[3,384,256]{2,1,0:T(8,128)(2,1)S(1)}, u32[]{:S(2)}, u32[]{:S(2)}) collective-permute-start(bf16[3,384,256]{2,1,0:T(8,128)(2,1)S(1)} %add_convert_fusion.1), channel_id=1, source_target_pairs={{0,6},{2,0},{4,2},{6,4},{1,7},{3,1},{5,3},{7,5},{8,14},{10,8},{12,... | collective-permute-start | bytes 1769480 | tf_op jit(solution)/shard_map/ppermute | solution.py:1036
  378.9 32.6 %collective-permute-start.71 = (bf16[96,1280]{1,0:T(8,128)(2,1)S(1)}, bf16[96,1280]{1,0:T(8,128)(2,1)S(1)}, u32[]{:S(2)}, u32[]{:S(2)}) collective-permute-start(bf16[96,1280]{1,0:T(8,128)(2,1)S(1)} %copy-done.51), channel_id=1, source_target_pairs={{0,2},{2,4},{4,6},{6,0},{1,3},{3,5},{5,7},{7,1},{8,10},{10,12},{12... | collective-permute-start | bytes 737288 | tf_op jit(solution)/shard_map/ppermute | solution.py:1032
  379.4 33.4 %collective-permute-start.74 = (bf16[96,1280]{1,0:T(8,128)(2,1)S(1)}, bf16[96,1280]{1,0:T(8,128)(2,1)S(1)}, u32[]{:S(2)}, u32[]{:S(2)}) collective-permute-start(bf16[96,1280]{1,0:T(8,128)(2,1)S(1)} %copy-done.50), channel_id=1, source_target_pairs={{0,6},{2,0},{4,2},{6,4},{1,7},{3,1},{5,3},{7,5},{8,14},{10,8},{12,... | collective-permute-start | bytes 737288 | tf_op jit(solution)/shard_map/ppermute | solution.py:1036
  427.8 30.0 %collective-permute-start.78 = (bf16[96,1280]{1,0:T(8,128)(2,1)S(1)}, bf16[96,1280]{1,0:T(8,128)(2,1)S(1)}, u32[]{:S(2)}, u32[]{:S(2)}) collective-permute-start(bf16[96,1280]{1,0:T(8,128)(2,1)S(1)} %fusion.3), channel_id=1, source_target_pairs={{0,16},{8,24},{16,0},{24,8},{1,17},{9,25},{17,1},{25,9},{2,18},{10... | collective-permute-start | bytes 737288 | tf_op jit(solution)/shard_map/ppermute | solution.py:1044
  (148 other events, 1946.6 us)
